TPU v7x, 32 devices: a whole 2x2x4 slice. The times are simulated.
32 devices in a mesh: section: 4 (over y, x), dp: 8 (over z, core).
Axes of the slice: x: 2, y: 2, z: 4, core: 2. Of those that a mesh axis runs over, the one named last changes fastest.
Arguments:
- ids: int32 [4, 1280, 32], P('section', 'dp'), may hold values from 0 to 49151, as said below
- masks: int32 [4, 1280, 32], P(None, 'dp'), may hold values 0 or 1
- labels: int32 [4, 1280], P(None, 'dp'), may hold values 0 or 1
- table: float32 [49152, 160], P('dp'), may hold values from -6 to 6
- table_first: float32 [49152, 160], P('dp'), may hold values from -3.8146973e-06 to 3.8146973e-06
- table_second: float32 [49152, 160], P('dp'), may hold values from 2.746582e-15 to 4.3945313e-14
- null_tokens: float32 [32, 160], replicated, may hold values from -6 to 6
- null_first: float32 [32, 160], replicated, may hold values from -4.5776367e-05 to 4.5776367e-05
- null_second: float32 [32, 160], replicated, may hold values from 3.90625e-13 to 6.25e-12
- w_up: float32 [2, 768, 1536], P(None, 'dp'), may hold values from -0.21875 to 0.21875
- up_first: float32 [2, 768, 1536], P(None, 'dp'), may hold values from -6.1035156e-05 to 6.1035156e-05
- up_second: float32 [2, 768, 1536], P(None, 'dp'), may hold values from 8.7890627e-13 to 1.40625e-11
- w_down: float32 [2, 1536, 2560], P(None, 'dp'), may hold values from -0.15625 to 0.15625
- down_first: float32 [2, 1536, 2560], P(None, 'dp'), may hold values from -6.1035156e-05 to 6.1035156e-05
- down_second: float32 [2, 1536, 2560], P(None, 'dp'), may hold values from 8.7890627e-13 to 1.40625e-11
- w_top: float32 [5120, 2048], P('dp'), may hold values from -0.078125 to 0.078125
- top_first: float32 [5120, 2048], P('dp'), may hold values from -0.00015258789 to 0.00015258789
- top_second: float32 [5120, 2048], P('dp'), may hold values from 4.785156e-12 to 7.65625e-11
- gains: float32 [2, 928], replicated, may hold values from 0.5 to 1.5
- gains_first: float32 [2, 928], replicated, may hold values from -0.00024414062 to 0.00024414062
- gains_second: float32 [2, 928], replicated, may hold values from 9.765625e-12 to 1.5625e-10
- biases: float32 [2, 5024], replicated, may hold values from -1.5 to 1.5
- biases_first: float32 [2, 5024], replicated, may hold values from -0.00012207031 to 0.00012207031
- biases_second: float32 [2, 5024], replicated, may hold values from 2.4414062e-12 to 3.90625e-11
- mixers: float32 [2, 1280], replicated, may hold values from -1 to 1
- mixers_first: float32 [2, 1280], replicated, may hold values from -0.00024414062 to 0.00024414062
- mixers_second: float32 [2, 1280], replicated, may hold values from 9.765625e-12 to 1.5625e-10
- top_bias: float32 [2048], replicated, may hold values from -1.5 to 1.5
- top_bias_first: float32 [2048], replicated, may hold values from -0.00015258789 to 0.00015258789
- top_bias_second: float32 [2048], replicated, may hold values from 4.785156e-12 to 7.65625e-11
- head: float32 [2049], replicated, may hold values from -1.5 to 1.5
- head_first: float32 [2049], replicated, may hold values from -0.0068359375 to 0.0068359375
- head_second: float32 [2049], replicated, may hold values from 8.789063e-09 to 1.40625e-07
Outputs:
- losses: float32 [4, 1280], P('section', 'dp')
- input_grad: bfloat16 [4, 1280, 32, 160], P('section', 'dp')
- table_new: float32 [49152, 160], P('dp')
- table_first_new: float32 [49152, 160], P('dp')
- table_second_new: float32 [49152, 160], P('dp')
- null_new: float32 [32, 160], replicated
- null_first_new: float32 [32, 160], replicated
- null_second_new: float32 [32, 160], replicated
- up_new: float32 [2, 768, 1536], P(None, 'dp')
- up_first_new: float32 [2, 768, 1536], P(None, 'dp')
- up_second_new: float32 [2, 768, 1536], P(None, 'dp')
- down_new: float32 [2, 1536, 2560], P(None, 'dp')
- down_first_new: float32 [2, 1536, 2560], P(None, 'dp')
- down_second_new: float32 [2, 1536, 2560], P(None, 'dp')
- top_new: float32 [5120, 2048], P('dp')
- top_first_new: float32 [5120, 2048], P('dp')
- top_second_new: float32 [5120, 2048], P('dp')
- gains_new: float32 [2, 928], replicated
- gains_first_new: float32 [2, 928], replicated
- gains_second_new: float32 [2, 928], replicated
- biases_new: float32 [2, 5024], replicated
- biases_first_new: float32 [2, 5024], replicated
- biases_second_new: float32 [2, 5024], replicated
- mixers_new: float32 [2, 1280], replicated
- mixers_first_new: float32 [2, 1280], replicated
- mixers_second_new: float32 [2, 1280], replicated
- top_bias_new: float32 [2048], replicated
- top_bias_first_new: float32 [2048], replicated
- top_bias_second_new: float32 [2048], replicated
- head_new: float32 [2049], replicated
- head_first_new: float32 [2049], replicated
- head_second_new: float32 [2049], replicated
Inputs may be any that keep to these rules, and one draw needn't show every extreme that they name: Of the 5120 ids of one micro-batch on one index of dp (aligned blocks of ids), at most 1280 lie in the 6144 rows held by one index of dp, and in every block exactly 1280 do for some index.
All inputs are finite; a program needn't handle non-finite values. No bound on the sum of `masks` or of `labels` on one device may be relied on, other than what follows from the above.
Results may differ from a plain program's by a relative error of at most 0.022.
Values may be sent and summed in bfloat16 or wider, within the bound.
A program may use at most 640 MiB of HBM per device.

v0:
```python
import jax
import jax.numpy as jnp
from jax import lax
from jax.sharding import PartitionSpec as P

D = 160
FEATS = 32
OUT_TOK = 16
LCB_TOK = 16
FM_RANK = 24
MLP_HID = 1536
TOP_HID = 2048
STEP = 10


beta_one = 0.9
beta_two = 0.999
adam_eps = 1e-08
norm_eps = 1e-05


def for_sending(value):
    return jax.tree.map(lambda a: a.astype(jnp.bfloat16) if a.dtype == jnp.float32 else a, value)


def shifted(value, axis, by):
    devices = lax.axis_size(axis)
    pairs = [(i, i + by) for i in range(devices) if 0 <= i + by < devices]
    return lax.ppermute(value, axis, pairs)


def layer_norm(values, scales, offsets):
    center = jnp.mean(values, axis=-1, keepdims=True)
    spread = values - center
    variance = jnp.mean(spread * spread, axis=-1, keepdims=True)
    return spread * lax.rsqrt(variance + norm_eps) * scales + offsets


def silu_slope(values):
    sigmoid = jax.nn.sigmoid(values)
    return sigmoid * (1.0 + values * (1.0 - sigmoid))


def adam_step(values, grads, first, second, rate, decay):
    first_new = beta_one * first + (1.0 - beta_one) * grads
    second_new = beta_two * second + (1.0 - beta_two) * grads * grads
    first_hat = first_new / (1.0 - beta_one**STEP)
    second_hat = second_new / (1.0 - beta_two**STEP)
    values_new = values - rate * (first_hat / (jnp.sqrt(second_hat) + adam_eps) + decay * values)
    return (values_new, first_new, second_new)


def pack_rows(pieces, members, pack_size):
    flat = jnp.concatenate([piece.reshape(members, -1) for piece in pieces], axis=1)
    return jnp.pad(flat, ((0, 0), (0, pack_size - flat.shape[1])))


def split_rows(scale_row, offset_row, mixer_row):
    rows_in = FEATS * FM_RANK
    middle = rows_in + MLP_HID
    outer = middle + OUT_TOK * D
    projector = mixer_row[:rows_in].reshape(FEATS, FM_RANK).astype(jnp.bfloat16)
    compress = mixer_row[rows_in:].reshape(LCB_TOK, FEATS).astype(jnp.bfloat16)
    return (
        scale_row[:rows_in],
        scale_row[rows_in:],
        offset_row[:rows_in],
        offset_row[rows_in:middle],
        offset_row[middle:outer],
        offset_row[outer:],
        projector,
        compress,
    )


def layer_forward(inputs, up_copy, down_copy, scale_row, offset_row, mixer_row):
    scale_one, scale_two, offset_one, bias_one, bias_two, offset_two, projector, compress = (
        split_rows(scale_row, offset_row, mixer_row)
    )
    rows = inputs.shape[0]
    inner = jnp.einsum("bnd,nk->bdk", inputs, projector, preferred_element_type=jnp.float32).astype(
        jnp.bfloat16
    )
    crossed = jnp.einsum("bnd,bdk->bnk", inputs, inner, preferred_element_type=jnp.float32).reshape(
        rows, FEATS * FM_RANK
    )
    normed = layer_norm(crossed, scale_one, offset_one).astype(jnp.bfloat16)
    hidden_pre = jnp.dot(normed, up_copy, preferred_element_type=jnp.float32) + bias_one
    hidden = jax.nn.silu(hidden_pre).astype(jnp.bfloat16)
    branch = (jnp.dot(hidden, down_copy, preferred_element_type=jnp.float32) + bias_two).reshape(
        rows, OUT_TOK, D
    )
    linear = jnp.einsum("mn,bnd->bmd", compress, inputs, preferred_element_type=jnp.float32)
    summed = inputs.astype(jnp.float32) + jnp.concatenate([branch, linear], axis=1)
    return (
        layer_norm(summed, scale_two, offset_two),
        (inner, crossed, normed, hidden_pre, hidden, summed),
    )


def layer_backward(inputs, upstream, up_copy, down_copy, scale_row, offset_row, mixer_row):
    scale_one, scale_two, offset_one, bias_one, bias_two, offset_two, projector, compress = (
        split_rows(scale_row, offset_row, mixer_row)
    )
    rows = inputs.shape[0]
    _, stored = layer_forward(inputs, up_copy, down_copy, scale_row, offset_row, mixer_row)
    inner, crossed, normed, hidden_pre, hidden, summed = stored
    _, second_back = jax.vjp(layer_norm, summed, scale_two, offset_two)
    grad_sum, grad_scale_two, grad_offset_two = second_back(upstream.astype(jnp.float32))
    grad_branch = grad_sum[:, :OUT_TOK].reshape(rows, OUT_TOK * D).astype(jnp.bfloat16)
    grad_linear = grad_sum[:, OUT_TOK:].astype(jnp.bfloat16)
    grad_bias_two = jnp.sum(grad_branch.astype(jnp.float32), axis=0)
    grad_down = jnp.einsum("bh,bo->ho", hidden, grad_branch, preferred_element_type=jnp.float32)
    grad_hidden = jnp.einsum(
        "bo,ho->bh", grad_branch, down_copy, preferred_element_type=jnp.float32
    )
    grad_pre = (grad_hidden * silu_slope(hidden_pre)).astype(jnp.bfloat16)
    grad_bias_one = jnp.sum(grad_pre.astype(jnp.float32), axis=0)
    grad_up = jnp.einsum("bi,bh->ih", normed, grad_pre, preferred_element_type=jnp.float32)
    grad_normed = jnp.einsum("bh,ih->bi", grad_pre, up_copy, preferred_element_type=jnp.float32)
    _, first_back = jax.vjp(layer_norm, crossed, scale_one, offset_one)
    grad_crossed, grad_scale_one, grad_offset_one = first_back(grad_normed)
    grad_crossed = grad_crossed.reshape(rows, FEATS, FM_RANK).astype(jnp.bfloat16)
    grad_inner = jnp.einsum(
        "bnk,bnd->bdk", grad_crossed, inputs, preferred_element_type=jnp.float32
    ).astype(jnp.bfloat16)
    grad_projector = jnp.einsum(
        "bnd,bdk->nk", inputs, grad_inner, preferred_element_type=jnp.float32
    )
    grad_compress = jnp.einsum(
        "bmd,bnd->mn", grad_linear, inputs, preferred_element_type=jnp.float32
    )
    grad_inputs = grad_sum + jnp.einsum(
        "bnk,bdk->bnd", grad_crossed, inner, preferred_element_type=jnp.float32
    )
    grad_inputs = grad_inputs + jnp.einsum(
        "nk,bdk->bnd", projector, grad_inner, preferred_element_type=jnp.float32
    )
    grad_inputs = grad_inputs + jnp.einsum(
        "mn,bmd->bnd", compress, grad_linear, preferred_element_type=jnp.float32
    )
    grad_scales = jnp.concatenate([grad_scale_one, grad_scale_two])
    grad_offsets = jnp.concatenate([grad_offset_one, grad_bias_one, grad_bias_two, grad_offset_two])
    grad_mixers = jnp.concatenate([grad_projector.reshape(-1), grad_compress.reshape(-1)])
    return (
        grad_inputs.astype(jnp.bfloat16),
        grad_up,
        grad_down,
        grad_scales,
        grad_offsets,
        grad_mixers,
    )


def top_forward(inputs, top_copy, top_bias, head):
    flat = inputs.reshape(inputs.shape[0], FEATS * D)
    top_pre = jnp.dot(flat, top_copy, preferred_element_type=jnp.float32) + top_bias
    top_act = jax.nn.silu(top_pre)
    logits = jnp.sum(top_act * head[:TOP_HID], axis=1) + head[TOP_HID]
    return (flat, top_pre, top_act, logits)


def per_device(
    ids,
    masks,
    labels,
    table,
    table_first,
    table_second,
    null_tokens,
    null_first,
    null_second,
    w_up,
    up_first,
    up_second,
    w_down,
    down_first,
    down_second,
    w_top,
    top_first,
    top_second,
    gains,
    gains_first,
    gains_second,
    biases,
    biases_first,
    biases_second,
    mixers,
    mixers_first,
    mixers_second,
    top_bias,
    top_bias_first,
    top_bias_second,
    head,
    head_first,
    head_second,
):
    sections = lax.axis_size("section")
    members = lax.axis_size("dp")
    section_index = lax.axis_index("section")
    micro_count = masks.shape[0]
    batch_rows = masks.shape[1]
    total = micro_count * batch_rows * members
    up_size = w_up.shape[1] * w_up.shape[2]
    down_size = w_down.shape[1] * w_down.shape[2]
    top_size = w_top.shape[0] * w_top.shape[1]
    pack_size = max(top_size, up_size + down_size)

    def pack_copies(pieces):
        flat = jnp.concatenate([piece.astype(jnp.bfloat16).reshape(-1) for piece in pieces])
        return jnp.pad(flat, (0, pack_size - flat.shape[0]))

    own_pack = lax.switch(
        section_index,
        [
            lambda: jnp.zeros((pack_size,), jnp.bfloat16),
            lambda: pack_copies((w_up[0], w_down[0])),
            lambda: pack_copies((w_up[1], w_down[1])),
            lambda: pack_copies((w_top,)),
        ],
    )
    gathered = jax.tree.map(
        lambda part, own: part.astype(own.dtype),
        lax.all_gather(for_sending(own_pack), "dp", axis=0, tiled=True),
        own_pack,
    ).reshape(members, pack_size)

    def layer_weights():
        up_copy = gathered[:, :up_size].reshape(members * w_up.shape[1], w_up.shape[2])
        down_copy = gathered[:, up_size : up_size + down_size].reshape(
            members * w_down.shape[1], w_down.shape[2]
        )
        return (up_copy, down_copy)

    def top_weights():
        return gathered[:, :top_size].reshape(members * w_top.shape[0], w_top.shape[1])

    flat_ids = ids.reshape(-1)
    id_count = flat_ids.shape[0]
    capacity = 2 * id_count // members
    rows_dev = table.shape[0]
    owners = flat_ids // rows_dev
    local_rows = flat_ids - owners * rows_dev
    hits = (owners[:, None] == jnp.arange(members, dtype=jnp.int32)[None, :]).astype(jnp.int32)
    slots = jnp.sum(jnp.cumsum(hits, axis=0) * hits, axis=1) - 1
    requests = jnp.zeros((members, capacity), jnp.int32).at[owners, slots].set(local_rows)
    table_copy = table.astype(jnp.bfloat16)
    asked = lax.all_to_all(requests, "dp", split_axis=0, concat_axis=0, tiled=True)
    found = jnp.take(table_copy, asked, axis=0)
    fetched = lax.all_to_all(found, "dp", split_axis=0, concat_axis=0, tiled=True)
    looked = fetched[owners, slots].reshape(1, batch_rows, FEATS, D)
    every_micro = lax.all_gather(looked, "section", axis=0, tiled=True)
    act_zero = jnp.zeros((batch_rows, FEATS, D), jnp.bfloat16)
    loss_zero = jnp.zeros((batch_rows,), jnp.float32)

    def run_fill(received, which_micro):
        rows_here = lax.dynamic_index_in_dim(every_micro, which_micro, 0, keepdims=False)
        present = lax.dynamic_index_in_dim(masks, which_micro, 0, keepdims=False) > 0
        filled = jnp.where(
            present[..., None], rows_here.astype(jnp.float32), null_tokens[None, :, :]
        )
        return (filled.astype(jnp.bfloat16), loss_zero)

    def run_layer(depth):

        def forward(received, which_micro):
            up_copy, down_copy = layer_weights()
            output, _ = layer_forward(
                received, up_copy, down_copy, gains[depth], biases[depth], mixers[depth]
            )
            return (output.astype(jnp.bfloat16), loss_zero)

        return forward

    def run_top(received, which_micro):
        _, _, _, logits = top_forward(received, top_weights(), top_bias, head)
        targets = lax.dynamic_index_in_dim(labels, which_micro, 0, keepdims=False).astype(
            jnp.float32
        )
        return (act_zero, jax.nn.softplus(logits) - targets * logits)

    def run_empty(received, which_micro):
        return (act_zero, loss_zero)

    forwards = [run_fill, run_layer(0), run_layer(1), run_top, run_empty]
    received = act_zero
    stash = jnp.zeros((micro_count, batch_rows, FEATS, D), jnp.bfloat16)
    loss_rows = jnp.zeros((micro_count, batch_rows), jnp.float32)
    for timestep in range(micro_count + sections - 1):
        position = timestep - section_index
        active = (position >= 0) & (position < micro_count)
        which_micro = jnp.clip(position, 0, micro_count - 1)
        chosen = jnp.where(active, section_index, sections)
        current = lax.dynamic_index_in_dim(stash, which_micro, 0, keepdims=False)
        stash = lax.dynamic_update_index_in_dim(
            stash, jnp.where(active, received, current), which_micro, 0
        )
        sent, loss_part = lax.switch(chosen, forwards, received, which_micro)
        previous = lax.dynamic_index_in_dim(loss_rows, which_micro, 0, keepdims=False)
        loss_rows = lax.dynamic_update_index_in_dim(
            loss_rows,
            jnp.where(active & (section_index == sections - 1), loss_part, previous),
            which_micro,
            0,
        )
        received = jax.tree.map(
            lambda part, own: part.astype(own.dtype), shifted(for_sending(sent), "section", 1), sent
        )

    def back_fill(stored, upstream, which_micro, packed, smalls):
        present = lax.dynamic_index_in_dim(masks, which_micro, 0, keepdims=False) > 0
        grad_rows = jnp.where(present[..., None], upstream, jnp.zeros_like(upstream))
        grad_null = jnp.sum(
            jnp.where(present[..., None], 0.0, upstream.astype(jnp.float32)), axis=0
        )
        return (grad_rows, packed, (smalls[0] + grad_null,) + smalls[1:])

    def back_layer(depth):

        def backward(stored, upstream, which_micro, packed, smalls):
            up_copy, down_copy = layer_weights()
            grad_inputs, grad_up, grad_down, grad_scales, grad_offsets, grad_mixers = (
                layer_backward(
                    stored, upstream, up_copy, down_copy, gains[depth], biases[depth], mixers[depth]
                )
            )
            packed = packed + pack_rows((grad_up, grad_down), members, pack_size)
            smalls = (
                smalls[0],
                smalls[1].at[depth].add(grad_scales),
                smalls[2].at[depth].add(grad_offsets),
                smalls[3].at[depth].add(grad_mixers),
            ) + smalls[4:]
            return (grad_inputs, packed, smalls)

        return backward

    def back_top(stored, upstream, which_micro, packed, smalls):
        top_copy = top_weights()
        flat, top_pre, top_act, logits = top_forward(stored, top_copy, top_bias, head)
        targets = lax.dynamic_index_in_dim(labels, which_micro, 0, keepdims=False).astype(
            jnp.float32
        )
        grad_logits = (jax.nn.sigmoid(logits) - targets) / total
        grad_head = jnp.concatenate(
            [jnp.sum(top_act * grad_logits[:, None], axis=0), jnp.sum(grad_logits)[None]]
        )
        grad_pre = (grad_logits[:, None] * head[:TOP_HID] * silu_slope(top_pre)).astype(
            jnp.bfloat16
        )
        grad_bias = jnp.sum(grad_pre.astype(jnp.float32), axis=0)
        grad_weight = jnp.einsum("bi,bh->ih", flat, grad_pre, preferred_element_type=jnp.float32)
        grad_inputs = jnp.einsum(
            "bh,ih->bi", grad_pre, top_copy, preferred_element_type=jnp.float32
        )
        packed = packed + pack_rows((grad_weight,), members, pack_size)
        smalls = smalls[:4] + (smalls[4] + grad_bias, smalls[5] + grad_head)
        return (grad_inputs.reshape(stored.shape).astype(jnp.bfloat16), packed, smalls)

    def back_empty(stored, upstream, which_micro, packed, smalls):
        return (act_zero, packed, smalls)

    backwards = [back_fill, back_layer(0), back_layer(1), back_top, back_empty]
    smalls = (
        jnp.zeros_like(null_tokens),
        jnp.zeros_like(gains),
        jnp.zeros_like(biases),
        jnp.zeros_like(mixers),
        jnp.zeros_like(top_bias),
        jnp.zeros_like(head),
    )
    packed_sum = jnp.zeros((members, pack_size), jnp.float32)
    input_rows = jnp.zeros((micro_count, batch_rows, FEATS, D), jnp.bfloat16)
    upstream = act_zero
    for timestep in range(micro_count + sections - 1):
        position = timestep - (sections - 1 - section_index)
        active = (position >= 0) & (position < micro_count)
        which_micro = jnp.clip(position, 0, micro_count - 1)
        chosen = jnp.where(active, section_index, sections)
        stored = lax.dynamic_index_in_dim(stash, which_micro, 0, keepdims=False)
        grad_out, packed_sum, smalls = lax.switch(
            chosen, backwards, stored, upstream, which_micro, packed_sum, smalls
        )
        earlier = lax.dynamic_index_in_dim(input_rows, which_micro, 0, keepdims=False)
        input_rows = lax.dynamic_update_index_in_dim(
            input_rows, jnp.where(active & (section_index == 0), grad_out, earlier), which_micro, 0
        )
        upstream = jax.tree.map(
            lambda part, own: part.astype(own.dtype),
            shifted(for_sending(grad_out), "section", -1),
            grad_out,
        )
    reduced = lax.psum_scatter(packed_sum, "dp", scatter_dimension=0, tiled=True)
    every_section = jax.tree.map(
        lambda part, own: part.astype(own.dtype),
        lax.all_gather(for_sending(reduced), "section", axis=0, tiled=True),
        reduced,
    )
    up_grad = jnp.stack(
        [
            every_section[1 + depth, :up_size].reshape(w_up.shape[1], w_up.shape[2])
            for depth in range(2)
        ]
    )
    down_grad = jnp.stack(
        [
            every_section[1 + depth, up_size : up_size + down_size].reshape(
                w_down.shape[1], w_down.shape[2]
            )
            for depth in range(2)
        ]
    )
    top_grad = every_section[3, :top_size].reshape(w_top.shape)
    small_total = lax.psum(smalls, ("section", "dp"))
    arrived_inputs = lax.all_to_all(input_rows, "section", split_axis=0, concat_axis=0, tiled=True)
    input_grad = arrived_inputs[0:1]
    grad_rows = input_grad.reshape(id_count, D)
    outgoing = jnp.zeros((members, capacity, D), jnp.bfloat16).at[owners, slots].set(grad_rows)
    arrived_rows = lax.all_to_all(outgoing, "dp", split_axis=0, concat_axis=0, tiled=True)
    table_part = (
        jnp.zeros((rows_dev, D), jnp.float32)
        .at[asked.reshape(-1)]
        .add(arrived_rows.reshape(-1, D).astype(jnp.float32))
    )
    table_grad = lax.psum(table_part.astype(jnp.bfloat16), "section").astype(jnp.float32)
    losses = lax.all_to_all(loss_rows, "section", split_axis=0, concat_axis=0, tiled=True)[
        sections - 1 : sections
    ]
    table_out = adam_step(table, table_grad, table_first, table_second, 1.0, 0.0)
    null_out = adam_step(null_tokens, small_total[0], null_first, null_second, 1.0, 0.0)
    up_out = adam_step(w_up, up_grad, up_first, up_second, 0.05, 0.01)
    down_out = adam_step(w_down, down_grad, down_first, down_second, 0.05, 0.01)
    top_out = adam_step(w_top, top_grad, top_first, top_second, 0.05, 0.01)
    gains_out = adam_step(gains, small_total[1], gains_first, gains_second, 1.0, 0.0)
    biases_out = adam_step(biases, small_total[2], biases_first, biases_second, 0.1, 0.0)
    mixers_out = adam_step(mixers, small_total[3], mixers_first, mixers_second, 0.2, 0.01)
    top_bias_out = adam_step(top_bias, small_total[4], top_bias_first, top_bias_second, 0.1, 0.0)
    head_out = adam_step(head, small_total[5], head_first, head_second, 0.1, 0.0)
    return (
        losses,
        input_grad,
        table_out[0],
        table_out[1],
        table_out[2],
        null_out[0],
        null_out[1],
        null_out[2],
        up_out[0],
        up_out[1],
        up_out[2],
        down_out[0],
        down_out[1],
        down_out[2],
        top_out[0],
        top_out[1],
        top_out[2],
        gains_out[0],
        gains_out[1],
        gains_out[2],
        biases_out[0],
        biases_out[1],
        biases_out[2],
        mixers_out[0],
        mixers_out[1],
        mixers_out[2],
        top_bias_out[0],
        top_bias_out[1],
        top_bias_out[2],
        head_out[0],
        head_out[1],
        head_out[2],
    )


def solution(mesh):
    placed = (
        P("section", "dp", None),
        P(None, "dp", None),
        P(None, "dp"),
        P("dp", None),
        P("dp", None),
        P("dp", None),
        P(),
        P(),
        P(),
        P(None, "dp", None),
        P(None, "dp", None),
        P(None, "dp", None),
        P(None, "dp", None),
        P(None, "dp", None),
        P(None, "dp", None),
        P("dp", None),
        P("dp", None),
        P("dp", None),
        P(),
        P(),
        P(),
        P(),
        P(),
        P(),
        P(),
        P(),
        P(),
        P(),
        P(),
        P(),
        P(),
        P(),
        P(),
    )
    return jax.shard_map(
        per_device,
        mesh=mesh,
        in_specs=placed,
        out_specs=(
            P("section", "dp"),
            P("section", "dp", None, None),
            P("dp", None),
            P("dp", None),
            P("dp", None),
            P(),
            P(),
            P(),
            P(None, "dp", None),
            P(None, "dp", None),
            P(None, "dp", None),
            P(None, "dp", None),
            P(None, "dp", None),
            P(None, "dp", None),
            P("dp", None),
            P("dp", None),
            P("dp", None),
            P(),
            P(),
            P(),
            P(),
            P(),
            P(),
            P(),
            P(),
            P(),
            P(),
            P(),
            P(),
            P(),
            P(),
            P(),
        ),
        check_vma=False,
    )
```

profile of v0, /device:TPU:0, one launch (start us, length us, event | category | flops | bytes accessed | tf_op | source)
XLA Modules:
  0.0 4598.7 jit_solution(14438618621670156719)
XLA Ops:
  15.2 19.8 scatter_custom_fusion.1
  35.1 6.3 all-to-all-start
  48.1 41.2 gather_fusion
  89.3 7.3 copy.1106
  98.8 79.3 %all_to_all.42 = bf16[8,1280,160]{1,2,0:T(8,128)(2,1)} all-to-all(bf16[8,1280,160]{1,2,0:T(8,128)(2,1)S(1)} %broadcast_select_fusion.6), channel_id=1, replica_groups=mesh['section'=4,'dp'=8] {'dp'}, dimensions={0} | all-to-all | bytes 6553600 | tf_op jit(solution)/shard_map/all_to_all | solution.py:250
  178.1 7.2 copy.1107
  185.3 89.8 %gather_fusion.1 = bf16[5120,160]{1,0:T(8,128)(2,1)} fusion(bf16[8,1280,160]{2,1,0:T(8,128)(2,1)} %copy.1107, s32[5120]{0:T(1024)S(1)} %bitcast.1401), kind=kCustom, calls=%fused_computation.1 | custom fusion | bytes 3317760 | tf_op jit(solution)/shard_map/gather | solution.py:251
  277.2 102.0 %all-gather.5.cloned.1.call-done = bf16[4,160,32,160]{3,2,1,0:T(8,128)(2,1)} async-done(((bf16[1,160,32,160]{3,2,1,0:T(8,128)(2,1)}), bf16[4,160,32,160]{3,2,1,0:T(8,128)(2,1)}) %all-gather.5.cloned.1.call-update) | async-done | bytes 6553616 | tf_op jit(solution)/shard_map/all_gather | solution.py:252
  379.3 187.7 %all-gather.7.cloned.1.call-done = bf16[10485760]{0:T(1024)(128)(2,1)} async-done(((bf16[1310720]{0:T(1024)(128)(2,1)}), bf16[10485760]{0:T(1024)(128)(2,1)}) %all-gather.7.cloned.1.call-update) | async-done | bytes 20971536 | tf_op jit(solution)/shard_map/all_gather | solution.py:224
  567.0 22.7 reshape.4617
  589.7 19.4 conditional.16
  611.5 56.7 %collective-permute-done = bf16[160,32,160]{2,1,0:T(8,128)(2,1)S(1)} collective-permute-done((bf16[160,32,160]{2,1,0:T(8,128)(2,1)}, bf16[160,32,160]{2,1,0:T(8,128)(2,1)S(1)}, u32[]{:S(2)}, u32[]{:S(2)}) %collective-permute-start) | collective-permute-done | bytes 1638432 | tf_op jit(solution)/shard_map/ppermute | solution.py:29
  669.6 19.9 conditional.17
  689.6 50.3 %collective-permute-start.1 = (bf16[160,32,160]{2,1,0:T(8,128)(2,1)}, bf16[160,32,160]{2,1,0:T(8,128)(2,1)S(1)}, u32[]{:S(2)}, u32[]{:S(2)}) collective-permute-start(bf16[160,32,160]{2,1,0:T(8,128)(2,1)} %get-tuple-element.2123), channel_id=1, source_target_pairs={{0,8},{8,16},{16,24},{1,9},{9,17},{17,25},{2,10},{10,18},{18,26},{... | collective-permute-start | bytes 4915208 | tf_op jit(solution)/shard_map/ppermute | solution.py:29
  739.9 55.9 %collective-permute-done.1 = bf16[160,32,160]{2,1,0:T(8,128)(2,1)S(1)} collective-permute-done((bf16[160,32,160]{2,1,0:T(8,128)(2,1)}, bf16[160,32,160]{2,1,0:T(8,128)(2,1)S(1)}, u32[]{:S(2)}, u32[]{:S(2)}) %collective-permute-start.1) | collective-permute-done | bytes 1638432 | tf_op jit(solution)/shard_map/ppermute | solution.py:29
  797.3 19.9 conditional.18
  817.2 50.2 %collective-permute-start.2 = (bf16[160,32,160]{2,1,0:T(8,128)(2,1)}, bf16[160,32,160]{2,1,0:T(8,128)(2,1)S(1)}, u32[]{:S(2)}, u32[]{:S(2)}) collective-permute-start(bf16[160,32,160]{2,1,0:T(8,128)(2,1)} %get-tuple-element.2125), channel_id=1, source_target_pairs={{0,8},{8,16},{16,24},{1,9},{9,17},{17,25},{2,10},{10,18},{18,26},{... | collective-permute-start | bytes 4915208 | tf_op jit(solution)/shard_map/ppermute | solution.py:29
  867.4 54.9 %collective-permute-done.2 = bf16[160,32,160]{2,1,0:T(8,128)(2,1)S(1)} collective-permute-done((bf16[160,32,160]{2,1,0:T(8,128)(2,1)}, bf16[160,32,160]{2,1,0:T(8,128)(2,1)S(1)}, u32[]{:S(2)}, u32[]{:S(2)}) %collective-permute-start.2) | collective-permute-done | bytes 1638432 | tf_op jit(solution)/shard_map/ppermute | solution.py:29
  923.9 19.9 conditional.19
  943.8 50.2 %collective-permute-start.3 = (bf16[160,32,160]{2,1,0:T(8,128)(2,1)}, bf16[160,32,160]{2,1,0:T(8,128)(2,1)S(1)}, u32[]{:S(2)}, u32[]{:S(2)}) collective-permute-start(bf16[160,32,160]{2,1,0:T(8,128)(2,1)} %get-tuple-element.2127), channel_id=1, source_target_pairs={{0,8},{8,16},{16,24},{1,9},{9,17},{17,25},{2,10},{10,18},{18,26},{... | collective-permute-start | bytes 4915208 | tf_op jit(solution)/shard_map/ppermute | solution.py:29
  994.0 54.0 %collective-permute-done.3 = bf16[160,32,160]{2,1,0:T(8,128)(2,1)S(1)} collective-permute-done((bf16[160,32,160]{2,1,0:T(8,128)(2,1)}, bf16[160,32,160]{2,1,0:T(8,128)(2,1)S(1)}, u32[]{:S(2)}, u32[]{:S(2)}) %collective-permute-start.3) | collective-permute-done | bytes 1638432 | tf_op jit(solution)/shard_map/ppermute | solution.py:29
  1049.5 22.2 conditional.20
  1071.7 50.8 %collective-permute-start.4 = (bf16[160,32,160]{2,1,0:T(8,128)(2,1)}, bf16[160,32,160]{2,1,0:T(8,128)(2,1)S(1)}, u32[]{:S(2)}, u32[]{:S(2)}) collective-permute-start(bf16[160,32,160]{2,1,0:T(8,128)(2,1)} %get-tuple-element.2129), channel_id=1, source_target_pairs={{0,8},{8,16},{16,24},{1,9},{9,17},{17,25},{2,10},{10,18},{18,26},{... | collective-permute-start | bytes 4915208 | tf_op jit(solution)/shard_map/ppermute | solution.py:29
  1132.2 43.4 collective-permute-done.4
  1177.1 23.9 conditional.21
  1222.4 35.2 collective-permute-done.5
  1261.8 12.9 dynamic-slice_bitcast_fusion
  1274.7 48.1 %conditional.23 = (bf16[160,32,160]{2,1,0:T(8,128)(2,1)}, f32[8,1310720]{1,0:T(8,128)}, f32[2,928]{1,0:T(2,128)S(1)}, f32[2,5024]{1,0:T(2,128)S(1)}, f32[2,1280]...) conditional(s32[]{:T(128)} %clamp.53, () %tuple.512, ...), branch_computations={%region_98.99_spmd, %region_99.113_spmd, %region_113.127_spmd, %re... | conditional | flops 10074356736 | bytes 358290432 | solution.py:381
  1302.3 13.6 broadcast_in_dim.637
  1324.8 100.6 %collective-permute-done.6 = bf16[160,32,160]{2,1,0:T(8,128)(2,1)S(1)} collective-permute-done((bf16[160,32,160]{2,1,0:T(8,128)(2,1)}, bf16[160,32,160]{2,1,0:T(8,128)(2,1)S(1)}, u32[]{:S(2)}, u32[]{:S(2)}) %collective-permute-start.6) | collective-permute-done | bytes 1638432 | tf_op jit(solution)/shard_map/ppermute | solution.py:29
  1426.9 32.0 conditional.24
  1460.2 55.7 %collective-permute-done.7 = bf16[160,32,160]{2,1,0:T(8,128)(2,1)} collective-permute-done((bf16[160,32,160]{2,1,0:T(8,128)(2,1)}, bf16[160,32,160]{2,1,0:T(8,128)(2,1)}, u32[]{:S(2)}, u32[]{:S(2)}) %collective-permute-start.7) | collective-permute-done | bytes 1638432 | tf_op jit(solution)/shard_map/ppermute | solution.py:29
  1515.9 32.0 conditional.25
  1549.2 543.3 %collective-permute-done.8 = bf16[160,32,160]{2,1,0:T(8,128)(2,1)S(1)} collective-permute-done((bf16[160,32,160]{2,1,0:T(8,128)(2,1)}, bf16[160,32,160]{2,1,0:T(8,128)(2,1)S(1)}, u32[]{:S(2)}, u32[]{:S(2)}) %collective-permute-start.8) | collective-permute-done | bytes 1638432 | tf_op jit(solution)/shard_map/ppermute | solution.py:29
  2094.0 22.9 conditional.26
  2118.3 281.1 %collective-permute-done.9 = bf16[160,32,160]{2,1,0:T(8,128)(2,1)} collective-permute-done((bf16[160,32,160]{2,1,0:T(8,128)(2,1)}, bf16[160,32,160]{2,1,0:T(8,128)(2,1)}, u32[]{:S(2)}, u32[]{:S(2)}) %collective-permute-start.9) | collective-permute-done | bytes 1638432 | tf_op jit(solution)/shard_map/ppermute | solution.py:29
  2399.5 27.2 conditional.27
  2435.0 271.0 %collective-permute-done.10 = bf16[160,32,160]{2,1,0:T(8,128)(2,1)} collective-permute-done((bf16[160,32,160]{2,1,0:T(8,128)(2,1)}, bf16[160,32,160]{2,1,0:T(8,128)(2,1)}, u32[]{:S(2)}, u32[]{:S(2)}) %collective-permute-start.10) | collective-permute-done | bytes 1638432 | tf_op jit(solution)/shard_map/ppermute | solution.py:29
  2706.0 27.6 conditional.28
  2734.9 5.2 bitcast_dynamic-update-slice_fusion.3
  2756.7 252.3 %collective-permute-done.11 = bf16[160,32,160]{2,1,0:T(8,128)(2,1)} collective-permute-done((bf16[160,32,160]{2,1,0:T(8,128)(2,1)}, bf16[160,32,160]{2,1,0:T(8,128)(2,1)}, u32[]{:S(2)}, u32[]{:S(2)}) %collective-permute-start.11) | collective-permute-done | bytes 1638432 | tf_op jit(solution)/shard_map/ppermute | solution.py:29
  3009.0 28.4 conditional.29
  3037.5 5.3 bitcast_dynamic-update-slice_fusion
  3042.8 11.1 all-to-all-start.3
  3054.6 109.4 %all-to-all-done.3 = bf16[4,160,32,160]{3,2,1,0:T(8,128)(2,1)} async-done(((bf16[4,160,32,160]{3,2,1,0:T(8,128)(2,1)}), bf16[4,160,32,160]{3,2,1,0:T(8,128)(2,1)}, u32[]{:S(2)}, u32[]{:S(2)}) %all-to-all-start.3) | async-done | bytes 6553632 | tf_op jit(solution)/shard_map/all_to_all | solution.py:415
  3166.0 25.6 scatter_custom_fusion.2
  3191.7 7.3 copy.1120
  3202.6 859.3 %all-reduce.31 = bf16[8,1310720]{1,0:T(8,128)(2,1)} all-reduce(f32[8,1310720]{1,0:T(8,128)} %get-tuple-element.2182), channel_id=2, replica_groups=mesh['section'=4,'dp'=8] {'dp'}, use_global_device_ids=true, to_apply=%region_365.366.clone | all-reduce | flops 10485760 | bytes 62914560
  4062.0 5.9 copy.1205
  4067.8 65.3 %scatter_custom_fusion = f32[6144,160]{1,0:T(8,128)} fusion(s32[10240]{0:T(1024)S(1)} %bitcast.1530, f32[10240,160]{1,0:T(8,128)} %bitcast.1454, f32[]{:T(128)} %constant.2187.clone.1), kind=kCustom, calls=%fused_computation.1605 | custom fusion | flops 1638400 | bytes 3932672 | tf_op jit(solution)/shard_map/scatter-add | solution.py:423
  4133.2 5.0 copy.1124
  4138.2 11.6 all-gather.9.cloned.1.call-start
  4149.8 12.1 fusion.563
  4163.9 47.6 %all_to_all.43 = f32[4,1,160]{2,1,0:T(1,128)S(1)} all-to-all(f32[4,1,160]{2,1,0:T(1,128)S(1)} %constant_dynamic-update-slice_fusion), channel_id=1, replica_groups=mesh['section'=4,'dp'=8] {'section'}, dimensions={0} | all-to-all | bytes 5120 | tf_op jit(solution)/shard_map/all_to_all | solution.py:426
  4221.1 9.5 add_subtract_fusion
  4230.6 186.0 %all-gather.9.cloned.1.call-done = bf16[4,1,1310720]{2,1,0:T(2,128)(2,1)} async-done(((bf16[1,1,1310720]{2,1,0:T(2,128)(2,1)}), bf16[4,1,1310720]{2,1,0:T(2,128)(2,1)}) %all-gather.9.cloned.1.call-update) | async-done | bytes 10485776 | tf_op jit(solution)/shard_map/all_gather | solution.py:396
  4416.6 23.3 copy.1216
  4439.9 22.7 slice_reduce_fusion.157
  4462.6 7.3 slice_reduce_fusion.159
  4478.5 23.5 convert_element_type.1571
  4502.0 56.5 %slice_reduce_fusion.156 = f32[1310720]{0:T(1024)} fusion(f32[4,1,1310720]{2,1,0:T(1,128)S(1)} %convert_element_type.1571), kind=kLoop, calls=%fused_computation.1592 | loop fusion | bytes 10485760 | tf_op jit(solution)/shard_map/slice | solution.py:413
  4558.5 6.7 reshape_squeeze.3
  4568.6 11.6 multiply_subtract_fusion.1
  4582.8 8.9 multiply_subtract_fusion
  (358 shorter events, 191.3 us)
Async XLA Ops:
  35.1 13.0 all-to-all-start
  41.4 337.9 %all-gather.5.cloned.1.call-start = ((), (), s32[]{:S(2)}) async-start(), calls=%async_computation.5 | async-start | bytes 13107200 | tf_op jit(solution)/shard_map/all_gather | solution.py:252
  48.0 48.5 %copy-start.254 = (s32[8,1,1280]{2,1,0:T(1,128)}, s32[8,1,1280]{2,1,0:T(1,128)S(1)}, u32[]{:S(2)}) copy-start(s32[8,1,1280]{2,1,0:T(1,128)S(1)} %all-to-all-done) | copy-start | bytes 122884
  275.1 291.9 %all-gather.7.cloned.1.call-start = ((), (), s32[]{:S(2)}) async-start(), calls=%async_computation.6 | async-start | bytes 23592960 | tf_op jit(solution)/shard_map/all_gather | solution.py:224
  379.2 210.4 %copy-start.76 = (s32[4,160,32]{1,2,0:T(8,128)S(1)}, s32[4,160,32]{1,2,0:T(8,128)}, u32[]{:S(2)}) copy-start(s32[4,160,32]{1,2,0:T(8,128)} %param.192) | copy-start | bytes 245764
  379.2 210.4 %copy-start.151 = (f32[2,5024]{1,0:T(2,128)S(1)}, f32[2,5024]{1,0:T(2,128)}, u32[]{:S(2)}) copy-start(f32[2,5024]{1,0:T(2,128)} %param.212) | copy-start | bytes 120580
  379.2 210.4 %copy-start.153 = (f32[2,1280]{1,0:T(2,128)S(1)}, f32[2,1280]{1,0:T(2,128)}, u32[]{:S(2)}) copy-start(f32[2,1280]{1,0:T(2,128)} %param.215) | copy-start | bytes 30724
  379.2 210.4 %copy-start.212 = (f32[32,160]{1,0:T(8,128)S(1)}, f32[32,160]{1,0:T(8,128)}, u32[]{:S(2)}) copy-start(f32[32,160]{1,0:T(8,128)} %param.197) | copy-start | bytes 61444
  379.2 210.4 %copy-start.220 = (f32[2,928]{1,0:T(2,128)S(1)}, f32[2,928]{1,0:T(2,128)}, u32[]{:S(2)}) copy-start(f32[2,928]{1,0:T(2,128)} %param.209) | copy-start | bytes 22276
  379.2 210.4 %copy-start.223 = (f32[2049]{0:T(1024)S(1)}, f32[2049]{0:T(1024)}, u32[]{:S(2)}) copy-start(f32[2049]{0:T(1024)} %param.221) | copy-start | bytes 24592
  379.3 210.4 %copy-start.294 = (s32[4,160]{1,0:T(4,128)S(1)}, s32[4,160]{1,0:T(4,128)}, u32[]{:S(2)}) copy-start(s32[4,160]{1,0:T(4,128)} %param.193) | copy-start | bytes 7684
  379.3 210.4 %copy-start.324 = (f32[2048]{0:T(1024)S(1)}, f32[2048]{0:T(1024)}, u32[]{:S(2)}) copy-start(f32[2048]{0:T(1024)} %param.218) | copy-start | bytes 24580
  609.1 59.1 %copy-start.348 = (f32[160]{0:T(256)}, f32[160]{0:T(256)S(1)}, u32[]{:S(2)}) copy-start(f32[160]{0:T(256)S(1)} %get-tuple-element.2120) | copy-start | bytes 1924
  609.1 59.1 %collective-permute-start = (bf16[160,32,160]{2,1,0:T(8,128)(2,1)}, bf16[160,32,160]{2,1,0:T(8,128)(2,1)S(1)}, u32[]{:S(2)}, u32[]{:S(2)}) collective-permute-start(bf16[160,32,160]{2,1,0:T(8,128)(2,1)} %get-tuple-element.2121), channel_id=1, source_target_pairs={{0,8},{8,16},{16,24},{1,9},{9,17},{17,25},{2,10},{10,18},{18,26},{... | collective-permute-start | bytes 4915208 | tf_op jit(solution)/shard_map/ppermute | solution.py:29
  689.6 106.2 %copy-start.338 = (f32[160]{0:T(256)}, f32[160]{0:T(256)S(1)}, u32[]{:S(2)}) copy-start(f32[160]{0:T(256)S(1)} %get-tuple-element.2122) | copy-start | bytes 1924
  689.6 106.2 %collective-permute-start.1 = (bf16[160,32,160]{2,1,0:T(8,128)(2,1)}, bf16[160,32,160]{2,1,0:T(8,128)(2,1)S(1)}, u32[]{:S(2)}, u32[]{:S(2)}) collective-permute-start(bf16[160,32,160]{2,1,0:T(8,128)(2,1)} %get-tuple-element.2123), channel_id=1, source_target_pairs={{0,8},{8,16},{16,24},{1,9},{9,17},{17,25},{2,10},{10,18},{18,26},{... | collective-permute-start | bytes 4915208 | tf_op jit(solution)/shard_map/ppermute | solution.py:29
  817.2 105.2 %copy-start.340 = (f32[160]{0:T(256)}, f32[160]{0:T(256)S(1)}, u32[]{:S(2)}) copy-start(f32[160]{0:T(256)S(1)} %get-tuple-element.2124) | copy-start | bytes 1924
  817.2 105.1 %collective-permute-start.2 = (bf16[160,32,160]{2,1,0:T(8,128)(2,1)}, bf16[160,32,160]{2,1,0:T(8,128)(2,1)S(1)}, u32[]{:S(2)}, u32[]{:S(2)}) collective-permute-start(bf16[160,32,160]{2,1,0:T(8,128)(2,1)} %get-tuple-element.2125), channel_id=1, source_target_pairs={{0,8},{8,16},{16,24},{1,9},{9,17},{17,25},{2,10},{10,18},{18,26},{... | collective-permute-start | bytes 4915208 | tf_op jit(solution)/shard_map/ppermute | solution.py:29
  943.8 104.2 %copy-start.342 = (f32[160]{0:T(256)}, f32[160]{0:T(256)S(1)}, u32[]{:S(2)}) copy-start(f32[160]{0:T(256)S(1)} %get-tuple-element.2126) | copy-start | bytes 1924
  943.8 104.2 %collective-permute-start.3 = (bf16[160,32,160]{2,1,0:T(8,128)(2,1)}, bf16[160,32,160]{2,1,0:T(8,128)(2,1)S(1)}, u32[]{:S(2)}, u32[]{:S(2)}) collective-permute-start(bf16[160,32,160]{2,1,0:T(8,128)(2,1)} %get-tuple-element.2127), channel_id=1, source_target_pairs={{0,8},{8,16},{16,24},{1,9},{9,17},{17,25},{2,10},{10,18},{18,26},{... | collective-permute-start | bytes 4915208 | tf_op jit(solution)/shard_map/ppermute | solution.py:29
  1071.7 52.2 %copy-start.344 = (f32[160]{0:T(256)}, f32[160]{0:T(256)S(1)}, u32[]{:S(2)}) copy-start(f32[160]{0:T(256)S(1)} %get-tuple-element.2128) | copy-start | bytes 1924
  1071.7 103.9 %collective-permute-start.4 = (bf16[160,32,160]{2,1,0:T(8,128)(2,1)}, bf16[160,32,160]{2,1,0:T(8,128)(2,1)S(1)}, u32[]{:S(2)}, u32[]{:S(2)}) collective-permute-start(bf16[160,32,160]{2,1,0:T(8,128)(2,1)} %get-tuple-element.2129), channel_id=1, source_target_pairs={{0,8},{8,16},{16,24},{1,9},{9,17},{17,25},{2,10},{10,18},{18,26},{... | collective-permute-start | bytes 4915208 | tf_op jit(solution)/shard_map/ppermute | solution.py:29
  1201.0 56.6 %collective-permute-start.5 = (bf16[160,32,160]{2,1,0:T(8,128)(2,1)}, bf16[160,32,160]{2,1,0:T(8,128)(2,1)S(1)}, u32[]{:S(2)}, u32[]{:S(2)}) collective-permute-start(bf16[160,32,160]{2,1,0:T(8,128)(2,1)} %get-tuple-element.2131), channel_id=1, source_target_pairs={{0,8},{8,16},{16,24},{1,9},{9,17},{17,25},{2,10},{10,18},{18,26},{... | collective-permute-start | bytes 4915208 | tf_op jit(solution)/shard_map/ppermute | solution.py:29
  1274.7 152.1 %copy-start.77 = (s32[4,160,32]{1,2,0:T(8,128)S(1)}, s32[4,160,32]{1,2,0:T(8,128)}, u32[]{:S(2)}) copy-start(s32[4,160,32]{1,2,0:T(8,128)} %param.192) | copy-start | bytes 245764
  1274.7 152.1 %copy-start.224 = (f32[2049]{0:T(1024)S(1)}, f32[2049]{0:T(1024)}, u32[]{:S(2)}) copy-start(f32[2049]{0:T(1024)} %param.221) | copy-start | bytes 24592
  1274.7 152.1 %copy-start.295 = (s32[4,160]{1,0:T(4,128)S(1)}, s32[4,160]{1,0:T(4,128)}, u32[]{:S(2)}) copy-start(s32[4,160]{1,0:T(4,128)} %param.193) | copy-start | bytes 7684
  1274.7 152.1 %copy-start.325 = (f32[2048]{0:T(1024)S(1)}, f32[2048]{0:T(1024)}, u32[]{:S(2)}) copy-start(f32[2048]{0:T(1024)} %param.218) | copy-start | bytes 24580
  1322.8 102.6 %copy-start.175 = (f32[2,5024]{1,0:T(2,128)}, f32[2,5024]{1,0:T(2,128)S(1)}, u32[]{:S(2)}) copy-start(f32[2,5024]{1,0:T(2,128)S(1)} %get-tuple-element.2136) | copy-start | bytes 120580
  1322.8 102.6 %copy-start.229 = (f32[2,1280]{1,0:T(2,128)}, f32[2,1280]{1,0:T(2,128)S(1)}, u32[]{:S(2)}) copy-start(f32[2,1280]{1,0:T(2,128)S(1)} %get-tuple-element.2137) | copy-start | bytes 30724
  1322.8 102.5 %copy-start.256 = (f32[2,928]{1,0:T(2,128)}, f32[2,928]{1,0:T(2,128)S(1)}, u32[]{:S(2)}) copy-start(f32[2,928]{1,0:T(2,128)S(1)} %get-tuple-element.2135) | copy-start | bytes 22276
  1322.9 102.5 %collective-permute-start.6 = (bf16[160,32,160]{2,1,0:T(8,128)(2,1)}, bf16[160,32,160]{2,1,0:T(8,128)(2,1)S(1)}, u32[]{:S(2)}, u32[]{:S(2)}) collective-permute-start(bf16[160,32,160]{2,1,0:T(8,128)(2,1)} %get-tuple-element.2132), channel_id=1, source_target_pairs={{8,0},{16,8},{24,16},{9,1},{17,9},{25,17},{10,2},{18,10},{26,18},{... | collective-permute-start | bytes 4915208 | tf_op jit(solution)/shard_map/ppermute | solution.py:29
  1426.8 89.0 %copy-start.9 = (bf16[160,32,160]{2,1,0:T(8,128)(2,1)S(1)}, bf16[160,32,160]{2,1,0:T(8,128)(2,1)}, u32[]{:S(2)}) copy-start(bf16[160,32,160]{2,1,0:T(8,128)(2,1)} %get-tuple-element.3448) | copy-start | bytes 4915204
  1426.9 89.0 %copy-start.221 = (f32[2,928]{1,0:T(2,128)S(1)}, f32[2,928]{1,0:T(2,128)}, u32[]{:S(2)}) copy-start(f32[2,928]{1,0:T(2,128)} %param.209) | copy-start | bytes 22276
  1458.9 57.0 %collective-permute-start.7 = (bf16[160,32,160]{2,1,0:T(8,128)(2,1)}, bf16[160,32,160]{2,1,0:T(8,128)(2,1)}, u32[]{:S(2)}, u32[]{:S(2)}) collective-permute-start(bf16[160,32,160]{2,1,0:T(8,128)(2,1)} %get-tuple-element.2140), channel_id=1, source_target_pairs={{8,0},{16,8},{24,16},{9,1},{17,9},{25,17},{10,2},{18,10},{26,18},{... | collective-permute-start | bytes 4915208 | tf_op jit(solution)/shard_map/ppermute | solution.py:29
  1547.9 544.6 %collective-permute-start.8 = (bf16[160,32,160]{2,1,0:T(8,128)(2,1)}, bf16[160,32,160]{2,1,0:T(8,128)(2,1)S(1)}, u32[]{:S(2)}, u32[]{:S(2)}) collective-permute-start(bf16[160,32,160]{2,1,0:T(8,128)(2,1)} %get-tuple-element.2148), channel_id=1, source_target_pairs={{8,0},{16,8},{24,16},{9,1},{17,9},{25,17},{10,2},{18,10},{26,18},{... | collective-permute-start | bytes 4915208 | tf_op jit(solution)/shard_map/ppermute | solution.py:29
  2094.0 305.4 %copy-start.2 = (bf16[160,32,160]{2,1,0:T(8,128)(2,1)S(1)}, bf16[160,32,160]{2,1,0:T(8,128)(2,1)}, u32[]{:S(2)}) copy-start(bf16[160,32,160]{2,1,0:T(8,128)(2,1)} %get-tuple-element.3446) | copy-start | bytes 4915204
  2117.0 282.5 %collective-permute-start.9 = (bf16[160,32,160]{2,1,0:T(8,128)(2,1)}, bf16[160,32,160]{2,1,0:T(8,128)(2,1)}, u32[]{:S(2)}, u32[]{:S(2)}) collective-permute-start(bf16[160,32,160]{2,1,0:T(8,128)(2,1)} %get-tuple-element.2156), channel_id=1, source_target_pairs={{8,0},{16,8},{24,16},{9,1},{17,9},{25,17},{10,2},{18,10},{26,18},{... | collective-permute-start | bytes 4915208 | tf_op jit(solution)/shard_map/ppermute | solution.py:29
  2426.7 279.3 %collective-permute-start.10 = (bf16[160,32,160]{2,1,0:T(8,128)(2,1)}, bf16[160,32,160]{2,1,0:T(8,128)(2,1)}, u32[]{:S(2)}, u32[]{:S(2)}) collective-permute-start(bf16[160,32,160]{2,1,0:T(8,128)(2,1)} %get-tuple-element.2164), channel_id=1, source_target_pairs={{8,0},{16,8},{24,16},{9,1},{17,9},{25,17},{10,2},{18,10},{26,18},{... | collective-permute-start | bytes 4915208 | tf_op jit(solution)/shard_map/ppermute | solution.py:29
  2433.2 272.8 %copy-start.37 = (bf16[4,160,32,160]{3,2,1,0:T(8,128)(2,1)}, bf16[4,160,32,160]{3,2,1,0:T(8,128)(2,1)S(1)}, u32[]{:S(2)}) copy-start(bf16[4,160,32,160]{3,2,1,0:T(8,128)(2,1)S(1)} %bitcast_dynamic-update-slice_fusion.4) | copy-start | bytes 19660804
  2433.2 272.8 %copy-start.1 = (bf16[160,32,160]{2,1,0:T(8,128)(2,1)S(1)}, bf16[160,32,160]{2,1,0:T(8,128)(2,1)}, u32[]{:S(2)}) copy-start(bf16[160,32,160]{2,1,0:T(8,128)(2,1)} %get-tuple-element.3445) | copy-start | bytes 4915204
  2433.2 272.8 %copy-start.222 = (f32[2,928]{1,0:T(2,128)S(1)}, f32[2,928]{1,0:T(2,128)}, u32[]{:S(2)}) copy-start(f32[2,928]{1,0:T(2,128)} %param.209) | copy-start | bytes 22276
  2433.3 272.7 %copy-start.225 = (f32[2049]{0:T(1024)S(1)}, f32[2049]{0:T(1024)}, u32[]{:S(2)}) copy-start(f32[2049]{0:T(1024)} %param.221) | copy-start | bytes 24592
  2433.3 272.7 %copy-start.296 = (s32[4,160]{1,0:T(4,128)S(1)}, s32[4,160]{1,0:T(4,128)}, u32[]{:S(2)}) copy-start(s32[4,160]{1,0:T(4,128)} %param.193) | copy-start | bytes 7684
  2433.3 272.7 %copy-start.326 = (f32[2048]{0:T(1024)S(1)}, f32[2048]{0:T(1024)}, u32[]{:S(2)}) copy-start(f32[2048]{0:T(1024)} %param.218) | copy-start | bytes 24580
  2733.6 275.4 %collective-permute-start.11 = (bf16[160,32,160]{2,1,0:T(8,128)(2,1)}, bf16[160,32,160]{2,1,0:T(8,128)(2,1)}, u32[]{:S(2)}, u32[]{:S(2)}) collective-permute-start(bf16[160,32,160]{2,1,0:T(8,128)(2,1)} %get-tuple-element.2172), channel_id=1, source_target_pairs={{8,0},{16,8},{24,16},{9,1},{17,9},{25,17},{10,2},{18,10},{26,18},{... | collective-permute-start | bytes 4915208 | tf_op jit(solution)/shard_map/ppermute | solution.py:29
  2753.1 256.0 %copy-start = (bf16[160,32,160]{2,1,0:T(8,128)(2,1)S(1)}, bf16[160,32,160]{2,1,0:T(8,128)(2,1)}, u32[]{:S(2)}) copy-start(bf16[160,32,160]{2,1,0:T(8,128)(2,1)} %get-tuple-element.3444) | copy-start | bytes 4915204
  2753.1 256.0 %copy-start.217 = (f32[32,160]{1,0:T(8,128)S(1)}, f32[32,160]{1,0:T(8,128)}, u32[]{:S(2)}) copy-start(f32[32,160]{1,0:T(8,128)} %get-tuple-element.2173) | copy-start | bytes 61444
  3042.8 121.2 %all-to-all-start.3 = ((bf16[4,160,32,160]{3,2,1,0:T(8,128)(2,1)}), bf16[4,160,32,160]{3,2,1,0:T(8,128)(2,1)}, u32[]{:S(2)}, u32[]{:S(2)}) async-start(bf16[4,160,32,160]{3,2,1,0:T(8,128)(2,1)} %bitcast_dynamic-update-slice_fusion), calls=%async_computation.3 | async-start | bytes 20971520 | tf_op jit(solution)/shard_map/all_to_all | solution.py:415
  3053.9 1158.2 %all-reduce.30.cloned.1.call-start = ((), (), s32[]{:S(2)}) async-start(), calls=%async_computation.9 | async-start | bytes 225280 | tf_op jit(solution)/shard_map/psum | solution.py:414
  3198.9 863.0 %all-to-all-start.4 = ((bf16[8,1280,160]{1,2,0:T(8,128)(2,1)}), bf16[8,1280,160]{1,2,0:T(8,128)(2,1)S(1)}, u32[]{:S(2)}, u32[]{:S(2)}) async-start(bf16[8,1280,160]{1,2,0:T(8,128)(2,1)} %copy.1120), calls=%async_computation.4 | async-start | bytes 6553600 | tf_op jit(solution)/shard_map/all_to_all | solution.py:419
  3202.6 1018.5 %all-reduce.28.cloned.1.call-start = ((), (), s32[]{:S(2)}) async-start(), calls=%async_computation.7 | async-start | bytes 3932160 | tf_op jit(solution)/shard_map/psum | solution.py:425
  4138.2 278.4 %all-gather.9.cloned.1.call-start = ((), (), s32[]{:S(2)}) async-start(), calls=%async_computation.8 | async-start | bytes 26214400 | tf_op jit(solution)/shard_map/all_gather | solution.py:396
  4163.7 49.7 %copy-start.330 = (f32[2,928]{1,0:T(2,128)S(1)}, f32[2,928]{1,0:T(2,128)}, u32[]{:S(2)}) copy-start(f32[2,928]{1,0:T(2,128)} %param.210) | copy-start | bytes 22276
  4163.7 49.7 %copy-start.331 = (f32[2,928]{1,0:T(2,128)S(1)}, f32[2,928]{1,0:T(2,128)}, u32[]{:S(2)}) copy-start(f32[2,928]{1,0:T(2,128)} %param.211) | copy-start | bytes 22276
  4163.7 51.0 %copy-start.316 = (f32[2049]{0:T(1024)S(1)}, f32[2049]{0:T(1024)}, u32[]{:S(2)}) copy-start(f32[2049]{0:T(1024)} %param.222) | copy-start | bytes 24592
  4163.7 51.0 %copy-start.317 = (f32[2049]{0:T(1024)S(1)}, f32[2049]{0:T(1024)}, u32[]{:S(2)}) copy-start(f32[2049]{0:T(1024)} %param.223) | copy-start | bytes 24592
  4163.7 52.4 %copy-start.213 = (f32[32,160]{1,0:T(8,128)S(1)}, f32[32,160]{1,0:T(8,128)}, u32[]{:S(2)}) copy-start(f32[32,160]{1,0:T(8,128)} %param.197) | copy-start | bytes 61444
  4163.8 52.3 %copy-start.311 = (f32[32,160]{1,0:T(8,128)S(1)}, f32[32,160]{1,0:T(8,128)}, u32[]{:S(2)}) copy-start(f32[32,160]{1,0:T(8,128)} %param.198) | copy-start | bytes 61444
  4163.8 52.3 %copy-start.312 = (f32[32,160]{1,0:T(8,128)S(1)}, f32[32,160]{1,0:T(8,128)}, u32[]{:S(2)}) copy-start(f32[32,160]{1,0:T(8,128)} %param.199) | copy-start | bytes 61444
  4163.8 53.7 %copy-start.318 = (f32[2,1280]{1,0:T(2,128)S(1)}, f32[2,1280]{1,0:T(2,128)}, u32[]{:S(2)}) copy-start(f32[2,1280]{1,0:T(2,128)} %param.216) | copy-start | bytes 30724
  4163.8 53.7 %copy-start.319 = (f32[2,1280]{1,0:T(2,128)S(1)}, f32[2,1280]{1,0:T(2,128)}, u32[]{:S(2)}) copy-start(f32[2,1280]{1,0:T(2,128)} %param.217) | copy-start | bytes 30724
  4163.8 55.1 %copy-start.152 = (f32[2,5024]{1,0:T(2,128)S(1)}, f32[2,5024]{1,0:T(2,128)}, u32[]{:S(2)}) copy-start(f32[2,5024]{1,0:T(2,128)} %param.212) | copy-start | bytes 120580
  4163.8 55.1 %copy-start.301 = (f32[2,5024]{1,0:T(2,128)S(1)}, f32[2,5024]{1,0:T(2,128)}, u32[]{:S(2)}) copy-start(f32[2,5024]{1,0:T(2,128)} %param.213) | copy-start | bytes 120580
  4163.8 55.0 %copy-start.302 = (f32[2,5024]{1,0:T(2,128)S(1)}, f32[2,5024]{1,0:T(2,128)}, u32[]{:S(2)}) copy-start(f32[2,5024]{1,0:T(2,128)} %param.214) | copy-start | bytes 120580
  (48 other events, 442.5 us)
Sparse Core Ops, SparseCore 0:
  275.2 103.9 all-gather.4
  381.4 185.4 all-gather.6
  3062.9 185.2 all-reduce.29
  4138.3 82.7 all-reduce.27
  4223.4 193.1 all-gather.8
where the time goes:
time: 4620 us; the launch traced here: 4600 us
  waiting for transfers between devices  2390 us (52%)
  blocking collectives  986 us (21%)
  local copies, waits for them, and re-layouts  460 us (10%)
  loops' own time  270 us (6%)
  starting transfers between devices  249 us (5%)
  other arithmetic  228 us (5%)
    ppermute x12, waiting for transfers between devices, shifted(): return lax.ppermute(value, axis, pairs)  1800 us
    unnamed x1, blocking collectives  859 us
    ppermute x12, starting transfers between devices, shifted(): return lax.ppermute(value, axis, pairs)  216 us
    all_gather x1, waiting for transfers between devices, per_device(): lax.all_gather(for_sending(own_pack), 'dp', axis=0, tiled=True)  188 us
    all_gather x1, waiting for transfers between devices, per_device(): lax.all_gather(for_sending(reduced), 'section', axis=0, tiled=True)  186 us
    another operation x7, loops' own time, per_device(): lax.switch(chosen, backwards, stored, upstream, which_micro, packed_sum,...  168 us
    all_to_all x1, waiting for transfers between devices, per_device(): lax.all_to_all(input_rows, 'section', split_axis=0, concat_axis=0, tiled=...  109 us
    unnamed x180, local copies, waits for them, and re-layouts  104 us
  transfers between devices with their start and end apart: 20, of which 17 were waited for; matrix products, arithmetic and copies ran while one was open for 4% of the time, Pallas kernels for 0%

commit v1 on v0

v1 whole, which is shorter than its diff:
```python
import functools

import jax
import jax.numpy as jnp
from jax import lax
from jax.experimental import pallas as pl
from jax.experimental.pallas import tpu as pltpu
from jax.sharding import PartitionSpec as P

D = 160
FEATS = 32
OUT_TOK = 16
LCB_TOK = 16
FM_RANK = 24
MLP_HID = 1536
TOP_HID = 2048
STEP = 10


beta_one = 0.9
beta_two = 0.999
adam_eps = 1e-08
norm_eps = 1e-05

MESH = pl.DeviceIdType.MESH
f32 = jnp.float32
bf16 = jnp.bfloat16


def layer_norm(values, scales, offsets):
    center = jnp.mean(values, axis=-1, keepdims=True)
    spread = values - center
    variance = jnp.mean(spread * spread, axis=-1, keepdims=True)
    return spread * lax.rsqrt(variance + norm_eps) * scales + offsets


def adam_step(values, grads, first, second, rate, decay):
    first_new = beta_one * first + (1.0 - beta_one) * grads
    second_new = beta_two * second + (1.0 - beta_two) * grads * grads
    first_hat = first_new / (1.0 - beta_one**STEP)
    second_hat = second_new / (1.0 - beta_two**STEP)
    values_new = values - rate * (first_hat / (jnp.sqrt(second_hat) + adam_eps) + decay * values)
    return (values_new, first_new, second_new)


def split_rows(scale_row, offset_row, mixer_row):
    rows_in = FEATS * FM_RANK
    middle = rows_in + MLP_HID
    outer = middle + OUT_TOK * D
    projector = mixer_row[:rows_in].reshape(FEATS, FM_RANK).astype(jnp.bfloat16)
    compress = mixer_row[rows_in:].reshape(LCB_TOK, FEATS).astype(jnp.bfloat16)
    return (
        scale_row[:rows_in],
        scale_row[rows_in:],
        offset_row[:rows_in],
        offset_row[rows_in:middle],
        offset_row[middle:outer],
        offset_row[outer:],
        projector,
        compress,
    )


def nn(a, b):
    return jnp.dot(a, b, preferred_element_type=f32)


def nt(a, b):
    return lax.dot_general(a, b, (((1,), (1,)), ((), ())), preferred_element_type=f32)


def row_sums(value):
    return jnp.sum(value.reshape(value.shape[0] // 8, 8, value.shape[1]), axis=0)


def all_sum(value):
    return jnp.sum(row_sums(value), axis=0, keepdims=True)


def same_example():
    side = FEATS * 8
    rows = lax.broadcasted_iota(jnp.int32, (side, side), 0)
    columns = lax.broadcasted_iota(jnp.int32, (side, side), 1)
    return (rows & 7) == (columns & 7)


def take_group(ref, start, half):
    pair = ref[:, pl.ds(pl.multiple_of(start, 16), 16), :].astype(f32)
    group = pair[:, 8 * half : 8 * half + 8, :]
    return group.reshape(group.shape[0] * 8, group.shape[2])


def silu_parts(value):
    sigmoid = 1.0 / (1.0 + jnp.exp(-value))
    return value * sigmoid, sigmoid * (1.0 + value * (1.0 - sigmoid))


def layer_copies(depth, up_hbm, down_hbm, up, down, up_sem, down_sem):
    copies = []
    for source, target, sem in ((up_hbm, up, up_sem), (down_hbm, down, down_sem)):
        rows = target.shape[1]
        if len(source.shape) == 3:
            source = source.at[:, pl.ds(depth * rows, rows), :]
        else:
            source = source.at[depth]
        copies.append([pltpu.make_async_copy(source, target, sem)])
    return copies


def all_rows(value):
    return value.reshape(value.shape[0] * value.shape[1], value.shape[2])


def forward_body(
    depth, x_ref, up_hbm, down_hbm, scale_one, offset_one, bias_one, bias_two, scale_two, offset_two, projector, compress,
    next_ref, summed_ref, crossed_ref, normed_back, pre_ref, hidden_back,
    up, down, mixed, linear, branch, normed_ref, hidden_ref, up_sem, down_sem,
):
    batch = x_ref.shape[1]
    up_copies, down_copies = layer_copies(depth, up_hbm, down_hbm, up, down, up_sem, down_sem)
    for copy in up_copies + down_copies:
        copy.start()
    mask = same_example()

    @pl.loop(0, batch // 16)
    def _(g):
        start = pl.multiple_of(g * 16, 16)
        for half in range(2):
            rows = take_group(x_ref, start, half).astype(bf16)
            gram = jnp.where(mask, nt(rows, rows), 0.0).astype(bf16)
            where = pl.ds(pl.multiple_of(start + 8 * half, 8), 8)
            mixed[:, where, :] = nn(gram, projector[...]).reshape(FEATS, 8, FM_RANK)
            linear[:, where, :] = nn(compress[...], rows).reshape(LCB_TOK, 8, D)

    for n in range(FEATS):
        crossed_ref[:, n * FM_RANK : (n + 1) * FM_RANK] = mixed[n]
    crossed = crossed_ref[...]
    normed = layer_norm(crossed, scale_one[...], offset_one[...])
    normed_ref[...] = normed.astype(bf16)
    normed_back[...] = normed.T.astype(bf16)
    for copy in up_copies:
        copy.wait()
    for j in range(0, MLP_HID, 256):
        columns = slice(j, j + 256)
        pre = nn(normed_ref[...], all_rows(up[:, :, columns])) + bias_one[:, columns]
        pre_ref[:, columns] = pre
        hidden = silu_parts(pre)[0]
        hidden_ref[:, columns] = hidden.astype(bf16)
        hidden_back[columns, :] = hidden.T.astype(bf16)
    for copy in down_copies:
        copy.wait()
    for j in range(0, OUT_TOK * D, 256):
        columns = slice(j, j + 256)
        branch[:, columns] = nn(hidden_ref[...], all_rows(down[:, :, columns])) + bias_two[:, columns]
    for n in range(OUT_TOK):
        summed_ref[n] = x_ref[n].astype(f32) + branch[:, n * D : (n + 1) * D]

    @pl.loop(OUT_TOK, FEATS)
    def _(n):
        summed_ref[n] = x_ref[n].astype(f32) + linear[n - OUT_TOK]

    @pl.loop(0, FEATS)
    def _(n):
        next_ref[n] = layer_norm(summed_ref[n], scale_two[...], offset_two[...]).astype(bf16)


def backward_body(
    depth, upstream, x_ref, summed, crossed_ref, pre_ref, up_hbm, down_hbm, scale_one, scale_two, projector, compress,
    compress_back,
    grad_x, branch_ref, grad_pre, scales_out, offsets_out, mixers_out,
    up, down, sums, branch, crossed_grad, mixed, scale_two_sum, offset_two_sum, projector_sum, compress_sum,
    up_sem, down_sem,
):
    batch = x_ref.shape[1]
    up_copies, down_copies = layer_copies(depth, up_hbm, down_hbm, up, down, up_sem, down_sem)
    for copy in down_copies + up_copies:
        copy.start()
    mask = same_example()
    rows_in = FEATS * FM_RANK
    middle = rows_in + MLP_HID
    scale_two_sum[...] = jnp.zeros_like(scale_two_sum)
    offset_two_sum[...] = jnp.zeros_like(offset_two_sum)
    projector_sum[...] = jnp.zeros_like(projector_sum)
    compress_sum[...] = jnp.zeros_like(compress_sum)

    @pl.loop(0, FEATS)
    def _(n):
        value = summed[n]
        above = upstream[n].astype(f32)
        spread = value - jnp.mean(value, axis=-1, keepdims=True)
        inverse = lax.rsqrt(jnp.mean(spread * spread, axis=-1, keepdims=True) + norm_eps)
        unit = spread * inverse
        scaled = above * scale_two[...]
        scale_two_sum[...] += row_sums(above * unit)
        offset_two_sum[...] += row_sums(above)
        sums[n] = inverse * (
            scaled
            - jnp.mean(scaled, axis=-1, keepdims=True)
            - unit * jnp.mean(scaled * unit, axis=-1, keepdims=True)
        )

    for n in range(OUT_TOK):
        branch[:, n * D : (n + 1) * D] = sums[n]
    for j in range(0, OUT_TOK * D, 256):
        columns = slice(j, j + 256)
        rounded = branch[:, columns].astype(bf16)
        branch_ref[:, columns] = rounded
        offsets_out[:, middle + j : middle + j + 256] = all_sum(rounded.astype(f32))
    for copy in down_copies:
        copy.wait()
    part_rows = down.shape[1]
    step = 2 * part_rows if down.shape[0] > 1 else 256
    for j in range(0, MLP_HID, step):
        columns = slice(j, j + step)
        if down.shape[0] > 1:
            weights = all_rows(down[j // part_rows : (j + step) // part_rows])
        else:
            weights = down[0, columns, :]
        below = nt(branch_ref[...], weights) * silu_parts(pre_ref[:, columns])[1]
        rounded = below.astype(bf16)
        grad_pre[:, columns] = rounded
        offsets_out[:, rows_in + j : rows_in + j + step] = all_sum(rounded.astype(f32))
    for copy in up_copies:
        copy.wait()
    crossed = crossed_ref[...]
    above = nt(grad_pre[...], all_rows(up[...]))
    spread = crossed - jnp.mean(crossed, axis=-1, keepdims=True)
    inverse = lax.rsqrt(jnp.mean(spread * spread, axis=-1, keepdims=True) + norm_eps)
    unit = spread * inverse
    scaled = above * scale_one[...]
    scales_out[:, :rows_in] = all_sum(above * unit)
    offsets_out[:, :rows_in] = all_sum(above)
    crossed_grad[...] = inverse * (
        scaled
        - jnp.mean(scaled, axis=-1, keepdims=True)
        - unit * jnp.mean(scaled * unit, axis=-1, keepdims=True)
    )
    for n in range(FEATS):
        mixed[n] = crossed_grad[:, n * FM_RANK : (n + 1) * FM_RANK]

    @pl.loop(0, batch // 16)
    def _(g):
        start = pl.multiple_of(g * 16, 16)
        parts = []
        for half in range(2):
            rows = take_group(x_ref, start, half).astype(bf16)
            where = pl.ds(pl.multiple_of(start + 8 * half, 8), 8)
            above = mixed[:, where, :].reshape(FEATS * 8, FM_RANK).astype(bf16)
            direct = sums[:, where, :].reshape(FEATS * 8, D)
            tail = direct[OUT_TOK * 8 :].astype(bf16)
            gram = jnp.where(mask, nt(rows, rows), 0.0).astype(bf16)
            projector_sum[...] += nn(gram, above)
            compress_sum[...] += nt(tail, rows)
            weights = projector[...]
            both = jnp.where(mask, nt(above, weights) + nt(weights, above), 0.0).astype(bf16)
            total = direct + nn(both, rows) + nn(compress_back[...], tail)
            parts.append(total.reshape(FEATS, 8, D))
        grad_x[:, pl.ds(start, 16), :] = jnp.concatenate(parts, axis=1).astype(bf16)

    scales_out[:, rows_in:] = jnp.sum(scale_two_sum[...], axis=0, keepdims=True)
    offsets_out[:, middle + OUT_TOK * D :] = jnp.sum(offset_two_sum[...], axis=0, keepdims=True)
    by_token = jnp.sum(projector_sum[...].reshape(FEATS, 8, FM_RANK), axis=1)
    for n in range(FEATS):
        mixers_out[:, n * FM_RANK : (n + 1) * FM_RANK] = by_token[n : n + 1]
    own_example = jnp.where(mask[: LCB_TOK * 8], compress_sum[...], 0.0)
    by_row = jnp.sum(own_example.reshape(LCB_TOK, 8, FEATS * 8), axis=1)
    side = FEATS * 8
    fold = lax.broadcasted_iota(jnp.int32, (side, FEATS), 0) // 8
    fold = (fold == lax.broadcasted_iota(jnp.int32, (side, FEATS), 1)).astype(f32)
    by_pair = jnp.dot(by_row, fold, preferred_element_type=f32, precision=lax.Precision.HIGHEST)
    for n in range(LCB_TOK):
        mixers_out[:, rows_in + n * FEATS : rows_in + (n + 1) * FEATS] = by_pair[n : n + 1]


def top_body(
    x_ref, weight_hbm, bias, head, targets, total,
    flat_back, logits_ref, grad_pre, grad_x, bias_out, head_out,
    weight, flat, flat_ref, pre, piece, sem,
):
    tile = 256
    copies = [
        pltpu.make_async_copy(
            weight_hbm.at[:, pl.ds(j * tile, tile)], weight.at[:, pl.ds(j * tile, tile)], sem.at[j]
        )
        for j in range(TOP_HID // tile)
    ]
    for copy in copies:
        copy.start()
    for n in range(FEATS):
        token = x_ref[n].astype(f32)
        flat[:, n * D : (n + 1) * D] = token
        flat_back[n * D : (n + 1) * D, :] = token.T.astype(bf16)
    for j in range(0, FEATS * D, 256):
        flat_ref[:, j : j + 256] = flat[:, j : j + 256].astype(bf16)
    logits = jnp.zeros((x_ref.shape[1], 1), f32)
    for j, copy in enumerate(copies):
        columns = slice(j * tile, (j + 1) * tile)
        copy.wait()
        value = nn(flat_ref[...], weight[:, columns]) + bias[:, columns]
        pre[:, columns] = value
        logits += jnp.sum(silu_parts(value)[0] * head[:, columns], axis=1, keepdims=True)
    logits = logits + head[:, TOP_HID : TOP_HID + 1]
    logits_ref[...] = logits
    grad_logits = (1.0 / (1.0 + jnp.exp(-logits)) - targets[...]) / total
    for j in range(0, TOP_HID, tile):
        columns = slice(j, j + tile)
        act, slope = silu_parts(pre[:, columns])
        rounded = (grad_logits * head[:, columns] * slope).astype(bf16)
        grad_pre[:, columns] = rounded
        bias_out[:, columns] = all_sum(rounded.astype(f32))
        head_out[:, columns] = all_sum(act * grad_logits)
    for j in range(0, FEATS, 4):
        piece[...] = nt(grad_pre[...], weight[j * D : (j + 4) * D, :])
        for k in range(4):
            grad_x[j + k] = piece[:, k * D : (k + 1) * D].astype(bf16)


def whole(count):
    return [pl.BlockSpec(memory_space=pltpu.VMEM)] * count


def in_place(count):
    return [pl.BlockSpec(memory_space=pl.ANY)] * count


def kernel_params():
    return pltpu.CompilerParams(vmem_limit_bytes=60 * 1024 * 1024)


def layer_values(scale_row, offset_row, mixer_row):
    scale_one, scale_two, offset_one, bias_one, bias_two, offset_two, projector, compress = split_rows(
        scale_row, offset_row, mixer_row
    )
    wide = jnp.repeat(projector, 8, axis=0)
    mixing = jnp.kron(compress.astype(f32), jnp.eye(8, dtype=f32)).astype(bf16)
    rows = [part[None, :] for part in (scale_one, offset_one, bias_one, bias_two, scale_two, offset_two)]
    return rows, wide, mixing


def layer_forward(depth, inputs, up_copy, down_copy, values):
    rows, wide, mixing = values
    batch = inputs.shape[1]
    parts = up_copy.shape[0] if len(up_copy.shape) == 3 else 1
    shape = jax.ShapeDtypeStruct
    return pl.pallas_call(
        functools.partial(forward_body, depth),
        out_shape=[
            shape((FEATS, batch, D), bf16),
            shape((FEATS, batch, D), f32),
            shape((batch, FEATS * FM_RANK), f32),
            shape((FEATS * FM_RANK, batch), bf16),
            shape((batch, MLP_HID), f32),
            shape((MLP_HID, batch), bf16),
        ],
        in_specs=whole(1) + in_place(2) + whole(8),
        out_specs=whole(6),
        scratch_shapes=[
            pltpu.VMEM((parts, FEATS * FM_RANK // parts, MLP_HID), bf16),
            pltpu.VMEM((parts, MLP_HID // parts, OUT_TOK * D), bf16),
            pltpu.VMEM((FEATS, batch, FM_RANK), f32),
            pltpu.VMEM((LCB_TOK, batch, D), f32),
            pltpu.VMEM((batch, OUT_TOK * D), f32),
            pltpu.VMEM((batch, FEATS * FM_RANK), bf16),
            pltpu.VMEM((batch, MLP_HID), bf16),
            pltpu.SemaphoreType.DMA(()),
            pltpu.SemaphoreType.DMA(()),
        ],
        compiler_params=kernel_params(),
        name="layer_forward",
    )(inputs, up_copy, down_copy, *rows, wide, mixing)


def layer_backward(depth, upstream, inputs, stored, up_copy, down_copy, values):
    rows, wide, mixing = values
    summed, crossed, normed, pre, hidden = stored
    batch = inputs.shape[1]
    parts = up_copy.shape[0] if len(up_copy.shape) == 3 else 1
    shape = jax.ShapeDtypeStruct
    outs = pl.pallas_call(
        functools.partial(backward_body, depth),
        out_shape=[
            shape((FEATS, batch, D), bf16),
            shape((batch, OUT_TOK * D), bf16),
            shape((batch, MLP_HID), bf16),
            shape((1, FEATS * FM_RANK + D), f32),
            shape((1, FEATS * FM_RANK + MLP_HID + OUT_TOK * D + D), f32),
            shape((1, FEATS * FM_RANK + LCB_TOK * FEATS), f32),
        ],
        in_specs=whole(5) + in_place(2) + whole(5),
        out_specs=whole(6),
        scratch_shapes=[
            pltpu.VMEM((parts, FEATS * FM_RANK // parts, MLP_HID), bf16),
            pltpu.VMEM((parts, MLP_HID // parts, OUT_TOK * D), bf16),
            pltpu.VMEM((FEATS, batch, D), f32),
            pltpu.VMEM((batch, OUT_TOK * D), f32),
            pltpu.VMEM((batch, FEATS * FM_RANK), f32),
            pltpu.VMEM((FEATS, batch, FM_RANK), f32),
            pltpu.VMEM((8, D), f32),
            pltpu.VMEM((8, D), f32),
            pltpu.VMEM((FEATS * 8, FM_RANK), f32),
            pltpu.VMEM((LCB_TOK * 8, FEATS * 8), f32),
            pltpu.SemaphoreType.DMA(()),
            pltpu.SemaphoreType.DMA(()),
        ],
        compiler_params=kernel_params(),
        name="layer_backward",
    )(upstream, inputs, summed, crossed, pre, up_copy, down_copy, rows[0], rows[4], wide, mixing, mixing.T)
    grad_x, grad_branch, grad_pre, scales, offsets, mixers = outs
    grad_up, grad_down = (normed, grad_pre), (hidden, grad_branch)
    return (
        grad_x,
        grad_up,
        grad_down,
        scales[0],
        offsets[0],
        mixers[0],
    )


def top_pass(inputs, top_copy, top_bias, head, targets, total):
    batch = inputs.shape[1]
    shape = jax.ShapeDtypeStruct
    flat, logits, grad_pre, grad_x, bias_sums, head_sums = pl.pallas_call(
        lambda *refs: top_body(*refs[:5], float(total), *refs[5:]),
        out_shape=[
            shape((FEATS * D, batch), bf16),
            shape((batch, 1), f32),
            shape((batch, TOP_HID), bf16),
            shape((FEATS, batch, D), bf16),
            shape((1, TOP_HID), f32),
            shape((1, TOP_HID), f32),
        ],
        in_specs=whole(1) + in_place(1) + whole(3),
        out_specs=whole(6),
        scratch_shapes=[
            pltpu.VMEM((FEATS * D, TOP_HID), bf16),
            pltpu.VMEM((batch, FEATS * D), f32),
            pltpu.VMEM((batch, FEATS * D), bf16),
            pltpu.VMEM((batch, TOP_HID), f32),
            pltpu.VMEM((batch, 4 * D), f32),
            pltpu.SemaphoreType.DMA((TOP_HID // 256,)),
        ],
        compiler_params=kernel_params(),
        name="top_pass",
    )(inputs, top_copy, top_bias[None, :], head[None, :], targets[:, None])
    logits = logits[:, 0]
    losses = jax.nn.softplus(logits) - targets * logits
    grad_logits = (jax.nn.sigmoid(logits) - targets) / total
    grad_head = jnp.concatenate([head_sums[0], jnp.sum(grad_logits)[None]])
    return losses, grad_x, (flat, grad_pre), bias_sums[0], grad_head


def gather_rows(matrix, section_index, sections, axis):
    rows = matrix.shape[axis] // sections
    piece = lax.dynamic_slice_in_dim(matrix, section_index * rows, rows, axis).astype(bf16)
    return lax.all_gather(piece, ("dp", "section"), axis=axis, tiled=True)


def chunk_rows(rows, weight, limit):
    best = rows
    for size in range(16, rows + 1, 16):
        if rows % size == 0 and (rows // size) % 2 == 0 and size * weight <= limit:
            best = size
    return best


def reduce_plan(shapes, members, plane_shapes):
    plan = []
    for index, (rows, cols) in enumerate(shapes):
        size = chunk_rows(rows, cols * members, 700000)
        plan += [(index, start, size, cols // 4, members // 2) for start in range(0, rows, size)]
    for index, (rows, cols) in enumerate(plane_shapes):
        size = chunk_rows(rows // 4, cols, 50000)
        plan += [
            (len(shapes) + index, start, size, cols, 1) for start in range(0, rows // 4, size)
        ]
    return plan


def ring_slots(plan):
    slots, ring, seen = [], [], {}
    for chunk in plan:
        *_, deep = chunk
        mine = seen.setdefault(chunk[2:], [])
        if deep == 1 or len(mine) < 6:
            ring.append(chunk)
            slots.append(len(ring) - 1)
        else:
            slots.append(mine[len(mine) % 6])
        mine.append(slots[-1])
    return slots, ring


def reduce_body(plan, slots, counts, members, *refs):
    matrices, planes, swaps, smalls = counts
    count = matrices + planes + swaps + smalls
    lefts, refs = refs[:matrices], refs[matrices:]
    inputs, outs, scratch = refs[:count], refs[count : 2 * count], refs[2 * count :]
    total = len(plan)
    stacks = members // 2
    ring = max(slots) + 1
    mixed, half = ([scratch[k * ring + slot] for slot in slots] for k in range(2))
    scratch = scratch[2 * ring :]
    first_in, second_in, quarter, done = (scratch[k * total : (k + 1) * total] for k in range(4))
    scratch = scratch[4 * total :]
    left, right, left_in, right_in = (scratch[k * matrices : (k + 1) * matrices] for k in range(4))
    stack_in = scratch[4 * matrices : 4 * matrices + sum(index < matrices for index, *_ in plan)]
    own_sem, side_sem, side_send, side_recv, pair_send, pair_recv, stack_send, stack_recv, out_send, out_recv, keep_sem, swap_send, swap_recv, swap_keep = (
        scratch[4 * matrices + len(stack_in) : 4 * matrices + len(stack_in) + 14]
    )
    small_now, small_in = scratch[-2 - 2 * smalls : -2 - smalls], scratch[-2 - smalls : -2]
    small_send, small_recv = scratch[-2:]
    section, member = lax.axis_index("section"), lax.axis_index("dp")
    stack, core = member // 2, member % 2
    x, y = section % 2, section // 2
    sibling = (section, member + 1 - 2 * core)
    beside_x = (section + 1 - 2 * x, member)
    beside_y = (section + 2 - 4 * y, member)
    others = [beside_x, beside_y, (3 - section, member)]
    peers = [(section, lax.rem(stack + k, stacks) * 2 + core) for k in range(1, stacks)]
    line = [(section, lax.rem(member + k, members)) for k in range(1, members)]

    barrier = pltpu.get_barrier_semaphore()
    partners = others + (line if swaps else [sibling] + peers)
    for device in partners:
        pl.semaphore_signal(barrier, inc=1, device_id=device, device_id_type=MESH)
    pl.semaphore_wait(barrier, len(partners))

    def remote(source, target, send, recv, device):
        return pltpu.make_async_remote_copy(
            src_ref=source, dst_ref=target, send_sem=send, recv_sem=recv, device_id=device, device_id_type=MESH
        )

    def own_copy(i):
        index, start, size, *_ = plan[i]
        return pltpu.make_async_copy(
            inputs[index].at[:, pl.ds(start, size), :], mixed[i], own_sem.at[i]
        )

    def side_copies(m):
        return [
            pltpu.make_async_copy(lefts[m].at[:, core], left[m], side_sem.at[m, 0]),
            pltpu.make_async_copy(inputs[m], right[m], side_sem.at[m, 1]),
            remote(lefts[m].at[:, 1 - core], left_in[m], side_send.at[m, 0], side_recv.at[m, 0], sibling),
            remote(inputs[m], right_in[m], side_send.at[m, 1], side_recv.at[m, 1], sibling),
        ]

    def first_copy(i):
        deep = plan[i][4]
        if i % 2 == 0:
            blocks = [(2 * t + 1 - x, t) for t in range(2)]
        else:
            blocks = [(2 * (1 - y) + t, t) for t in range(2)]
        return [
            remote(
                mixed[i].at[pl.ds(block * deep, deep)],
                first_in[i].at[t],
                pair_send.at[i, t],
                pair_recv.at[i, t],
                beside_x if i % 2 == 0 else beside_y,
            )
            for block, t in blocks
        ]

    def second_copy(i):
        source, device = (
            (half[i].at[1 - y], beside_y) if i % 2 == 0 else (half[i].at[1 - x], beside_x)
        )
        return remote(source, second_in[i], pair_send.at[i, 2], pair_recv.at[i, 2], device)

    def stack_copy(i, k):
        return remote(
            quarter[i].at[lax.rem(stack + k + 1, stacks)],
            stack_in[i].at[k],
            stack_send.at[i, k],
            stack_recv.at[i, k],
            peers[k],
        )

    def place(i, which):
        index, start, size, width, _ = plan[i]
        if index >= matrices:
            rows = outs[index].shape[0] // 4
            return outs[index].at[pl.ds(pl.multiple_of(which * rows + start, 16), size), :]
        columns = pl.ds(pl.multiple_of(which * width, 128), width)
        return outs[index].at[pl.ds(start, size), columns]

    def out_copy(i, k, arrived=False):
        first, second = (beside_x, beside_y) if i % 2 == 0 else (beside_y, beside_x)
        sent = place(i, (section, section, first[0])[k])
        came = place(i, (first[0], second[0], 3 - section)[k])
        source = sent if k == 2 else done[i]
        return remote(
            source, came if arrived else sent, out_send.at[i, k], out_recv.at[i, k], second if k else first
        )

    def keep_copy(i):
        return pltpu.make_async_copy(done[i], place(i, section), keep_sem.at[i])

    def swap_copy(j, k):
        index = matrices + planes + j
        return remote(
            inputs[index].at[lax.rem(member + k + 1, members)],
            outs[index].at[member],
            swap_send.at[j, k],
            swap_recv.at[j, k],
            line[k],
        )

    def swap_arrival(j, k):
        index = matrices + planes + j
        return remote(
            inputs[index].at[member],
            outs[index].at[lax.rem(member + members - k - 1, members)],
            swap_send.at[j, k],
            swap_recv.at[j, k],
            line[k],
        )

    def swap_own(j):
        index = matrices + planes + j
        return pltpu.make_async_copy(
            inputs[index].at[member], outs[index].at[member], swap_keep.at[j]
        )

    across_stacks = [
        (section, (stack + step - 2 * step * (stack // step % 2)) * 2 + core)
        for step in (1, 2, 4)
        if step < stacks
    ]
    pairs = [sibling, beside_x, beside_y] + across_stacks

    def small_copy(j, t):
        return remote(small_now[j], small_in[j].at[t], small_send.at[j, t], small_recv.at[j, t], pairs[t])

    def small_first(j):
        return pltpu.make_async_copy(inputs[count - smalls + j], small_now[j], small_send.at[j, 0])

    def small_last(j):
        return pltpu.make_async_copy(small_now[j], outs[count - smalls + j], small_send.at[j, 0])

    def stage_small(t):
        for j in range(smalls):
            if t == 0:
                small_first(j).wait()
            else:
                small_copy(j, t - 1).wait()
                small_now[j][...] += small_in[j][t - 1]
        for j in range(smalls):
            if t < len(pairs):
                small_copy(j, t).start()
            else:
                small_last(j).start()

    def stage_product(i):
        index, start, size, width, deep = plan[i]
        if index >= matrices:
            own_copy(i).wait()
        else:
            if start == 0:
                for copy in side_copies(index):
                    copy.wait()
            twice = i + 1 < total and plan[i + 1][:3] == (index, start + size, size)
            if start // size % 2 == 0:
                reach = 2 * size if twice else size
                rows = slice(start, start + reach)
                mine, other = all_rows(left[index][:, rows, :]), all_rows(left_in[index][:, rows, :])
                for s in range(4):
                    columns = slice(s * width, (s + 1) * width)
                    value = nn(mine, right[index][:, columns]) + nn(other, right_in[index][:, columns])
                    value = value.astype(bf16).reshape(deep, reach, width)
                    mixed[i][s * deep : (s + 1) * deep] = value[:, :size]
                    if twice:
                        mixed[i + 1][s * deep : (s + 1) * deep] = value[:, size:]

        for copy in first_copy(i):
            copy.start()

    def stage_first(i):
        deep = plan[i][4]
        for copy in first_copy(i):
            copy.wait()

        @pl.loop(0, deep)
        def _(z):
            for t in range(2):
                block = 2 * t + x if i % 2 == 0 else 2 * y + t
                mine = mixed[i][block * deep + z]
                half[i][t, z] = (mine.astype(f32) + first_in[i][t, z].astype(f32)).astype(bf16)

        second_copy(i).start()

    def stage_second(i):
        deep = plan[i][4]
        second_copy(i).wait()

        @pl.loop(0, deep)
        def _(z):
            mine = half[i][y, z] if i % 2 == 0 else half[i][x, z]
            quarter[i][z] = (mine.astype(f32) + second_in[i][z].astype(f32)).astype(bf16)

        for k in range(deep - 1):
            stack_copy(i, k).start()

    def stage_stack(i):
        deep = plan[i][4]
        for k in range(deep - 1):
            stack_copy(i, k).wait()
        value = quarter[i][stack if deep > 1 else 0].astype(f32)
        for k in range(deep - 1):
            value = value + stack_in[i][k].astype(f32)
        done[i][...] = value.astype(bf16)
        keep_copy(i).start()
        out_copy(i, 0).start()

    def stage_out(i):
        out_copy(i, 0, True).wait_recv()
        for k in (1, 2):
            out_copy(i, k).start()

    lag = 3
    for j in range(smalls):
        small_first(j).start()
    for m in range(matrices):
        for copy in side_copies(m):
            copy.start()
    for i in range(total):
        if plan[i][0] >= matrices:
            own_copy(i).start()
    for j in range(swaps):
        swap_own(j).start()
    patience = 6 if swaps else lag
    lags = (0, lag, 2 * lag, 2 * lag + patience, 3 * lag + patience)
    stages = tuple(zip(lags, (stage_product, stage_first, stage_second, stage_stack, stage_out)))
    for step in range(total + lags[-1]):
        if step % 4 == 0 and step // 4 < members - 1:
            for j in range(swaps):
                swap_copy(j, step // 4).start()
        for behind, stage in stages:
            if 0 <= step - behind < total:
                stage(step - behind)
        if smalls and step % 3 == 0 and step // 3 <= len(pairs):
            stage_small(step // 3)
    for i in range(total):
        keep_copy(i).wait()
        for k in range(3):
            out_copy(i, k).wait_send()
            if k:
                out_copy(i, k, True).wait_recv()
    for j in range(smalls):
        small_last(j).wait()
    for j in range(swaps):
        swap_own(j).wait()
        for k in range(members - 1):
            swap_copy(j, k).wait_send()
            swap_arrival(j, k).wait_recv()


def reduce_kernel(pairs, planes, swaps, smalls, members, collective_id):
    stacks = members // 2
    count = len(pairs)
    shapes = [(left.shape[0] // members, right.shape[1]) for left, right in pairs]
    plan = reduce_plan(shapes, members, [part.shape for part in planes])
    total, matrix_chunks = len(plan), sum(index < count for index, *_ in plan)
    lefts = [left.reshape(stacks, 2, -1, left.shape[1]) for left, _ in pairs]
    inputs = [right for _, right in pairs]
    inputs += [part.reshape((4, part.shape[0] // 4, part.shape[1])) for part in planes]
    inputs += list(swaps) + list(smalls)
    steps = 3 + (stacks - 1).bit_length()

    slots, ring = ring_slots(plan)

    def buffers(lead, chunks=plan):
        return [pltpu.VMEM(lead(deep) + (size, width), bf16) for _, _, size, width, deep in chunks]

    sides = [pltpu.VMEM((stacks,) + left.shape[2:], bf16) for left in lefts]
    sides += [pltpu.VMEM(right.shape, bf16) for _, right in pairs]
    across = [
        pltpu.VMEM((deep - 1, size, width), bf16) for _, _, size, width, deep in plan[:matrix_chunks]
    ]
    dma = pltpu.SemaphoreType.DMA
    swap_count = max(len(swaps), 1)
    return pl.pallas_call(
        functools.partial(
            reduce_body, plan, slots, (count, len(planes), len(swaps), len(smalls)), members
        ),
        out_shape=[jax.ShapeDtypeStruct(shape, bf16) for shape in shapes]
        + [jax.ShapeDtypeStruct(part.shape, part.dtype) for part in (*planes, *swaps, *smalls)],
        in_specs=in_place(count + len(inputs)),
        out_specs=in_place(len(inputs)),
        scratch_shapes=buffers(lambda deep: (4 * deep,), ring)
        + buffers(lambda deep: (2, deep), ring)
        + buffers(lambda deep: (2, deep))
        + buffers(lambda deep: (deep,)) * 2
        + buffers(lambda deep: ())
        + sides * 2
        + across
        + [
            dma((total,)),
            dma((max(count, 1), 2)),
            dma((max(count, 1), 2)),
            dma((max(count, 1), 2)),
            dma((total, 3)),
            dma((total, 3)),
            dma((total, stacks - 1)),
            dma((total, stacks - 1)),
            dma((total, 3)),
            dma((total, 3)),
            dma((total,)),
            dma((swap_count, members - 1)),
            dma((swap_count, members - 1)),
            dma((swap_count,)),
        ]
        + [pltpu.VMEM(part.shape, f32) for part in smalls]
        + [pltpu.VMEM((steps,) + part.shape, f32) for part in smalls]
        + [dma((max(len(smalls), 1), steps))] * 2,
        compiler_params=pltpu.CompilerParams(
            collective_id=collective_id, has_side_effects=True, vmem_limit_bytes=60 * 1024 * 1024
        ),
        name="reduce_rows",
    )(*lefts, *inputs)


MAIN = 128
TAIL = D - MAIN


def pack_body(members, slots, rows_ref, main_ref, tail_ref, main, tail):
    capacity = main_ref.shape[1]
    part = capacity // 4
    main[...] = jnp.zeros_like(main)
    tail[...] = jnp.zeros_like(tail)

    @pl.loop(0, rows_ref.shape[0] // 16)
    def _(i):
        start = pl.multiple_of(i * 16, 16)
        block = rows_ref[pl.ds(start, 16), :].astype(f32)
        for u in range(16):
            slot = pl.ds(slots[start + u], 1)
            main[slot, :] = block[u : u + 1, :MAIN]
            tail[slot, :] = block[u : u + 1, MAIN:]

    @pl.loop(0, members)
    def _(k):
        start = pl.multiple_of(k * capacity, 16)
        main_ref[k] = main[pl.ds(start, capacity), :].astype(bf16)
        pieces = [tail[pl.ds(start + j * part, part), :] for j in range(4)]
        tail_ref[k] = jnp.concatenate(pieces, axis=1).astype(bf16)


def pack_rows(rows, slots, members, capacity):
    shape = jax.ShapeDtypeStruct
    return pl.pallas_call(
        functools.partial(pack_body, members),
        out_shape=[shape((members, capacity, MAIN), bf16), shape((members, capacity // 4, MAIN), bf16)],
        in_specs=[pl.BlockSpec(memory_space=pltpu.SMEM)] + whole(1),
        out_specs=whole(2),
        scratch_shapes=[
            pltpu.VMEM((members * capacity, MAIN), f32),
            pltpu.VMEM((members * capacity, TAIL), f32),
        ],
        compiler_params=kernel_params(),
        name="pack_rows",
    )(slots, rows)


def add_body(members, asked, counts, main_ref, tail_ref, main_out, tail_out, main, tail, *sums):
    capacity = main_ref.shape[1]
    part = capacity // 4
    for total in sums:
        total[...] = jnp.zeros_like(total)

    @pl.loop(0, members)
    def _(k):
        start = pl.multiple_of(k * capacity, 16)
        main[pl.ds(start, capacity), :] = main_ref[k].astype(f32)
        wide = tail_ref[k].astype(f32)
        for j in range(4):
            tail[pl.ds(start + j * part, part), :] = wide[:, j * TAIL : (j + 1) * TAIL]

    @pl.loop(0, members)
    def _(k):
        @pl.loop(0, (counts[k] + 3) // 4)
        def _(i):
            for u in range(4):
                j = k * capacity + i * 4 + u
                here, there = pl.ds(j, 1), pl.ds(asked[j], 1)
                sums[2 * u][there, :] += main[here, :]
                sums[2 * u + 1][there, :] += tail[here, :]

    rows = main_out.shape[0] // 4
    tiles = []
    for j in range(4):
        where = slice(j * rows, (j + 1) * rows)
        main_out[where, :] = (
            sums[0][where, :] + sums[2][where, :] + sums[4][where, :] + sums[6][where, :]
        ).astype(bf16)
        tiles.append(sums[1][where, :] + sums[3][where, :] + sums[5][where, :] + sums[7][where, :])
    tail_out[...] = jnp.concatenate(tiles, axis=1).astype(bf16)


def add_rows(main, tail, asked, counts, rows):
    members, capacity, _ = main.shape
    shape = jax.ShapeDtypeStruct
    smem = pl.BlockSpec(memory_space=pltpu.SMEM)
    return pl.pallas_call(
        functools.partial(add_body, members),
        out_shape=[shape((rows, MAIN), bf16), shape((rows // 4, MAIN), bf16)],
        in_specs=[smem, smem] + whole(2),
        out_specs=whole(2),
        scratch_shapes=[
            pltpu.VMEM((members * capacity, MAIN), f32),
            pltpu.VMEM((members * capacity, TAIL), f32),
        ]
        + [pltpu.VMEM((rows, MAIN), f32), pltpu.VMEM((rows, TAIL), f32)] * 4,
        compiler_params=kernel_params(),
        name="add_rows",
    )(asked, counts, main, tail)


def gather_body(members, plan, counts, *refs):
    matrices, swaps = counts
    count = matrices + swaps
    inputs, outs = refs[:count], refs[count : 2 * count]
    next_send, pass_send, stack_recv, pair_send, pair_recv, core_send, core_recv, own_send, own_recv, keep, swap_send, swap_recv = (
        refs[2 * count :]
    )
    stacks = members // 2
    section, member = lax.axis_index("section"), lax.axis_index("dp")
    stack, core = member // 2, member % 2
    x, y = section % 2, section // 2
    sibling = (section, member + 1 - 2 * core)
    over_x, over_y = section + 1 - 2 * x, section + 2 - 4 * y
    line = [(section, lax.rem(member + k, members)) for k in range(1, members)]
    partners = [(over_x, member), (over_y, member)] + line
    barrier = pltpu.get_barrier_semaphore()
    for device in partners:
        pl.semaphore_signal(barrier, inc=1, device_id=device, device_id_type=MESH)
    pl.semaphore_wait(barrier, len(partners))

    def remote(source, target, send, recv, device):
        return pltpu.make_async_remote_copy(
            src_ref=source, dst_ref=target, send_sem=send, recv_sem=recv, device_id=device, device_id_type=MESH
        )

    pieces = len(plan)
    if stacks == 4:
        lowest, highest = 1 - (stack + 3) // 4, (stack + 1) // 4
        by_distance = [1 + 2 * lowest, 3 - lowest - highest, 2 - lowest + highest]
    else:
        by_distance = list(range(1, stacks))
    units = [(i, k) for i in range(pieces) for k in by_distance]

    def unit(i, k):
        return i * (stacks - 1) + k - 1

    def block(i, owner_stack, which_core, which_section):
        index, start, size, width = plan[i]
        owner = owner_stack * 2 + which_core
        if which_section is None:
            return outs[index].at[owner, pl.ds(start, size), :]
        columns = pl.ds(pl.multiple_of(which_section * width, 128), width)
        return outs[index].at[owner, pl.ds(start, size), columns]

    def from_stack_of(k):
        return lax.rem(stack + stacks - k, stacks)

    def beyond(up):
        return (section, member + (2 if up else -2))

    def next_copy(i, up):
        index, start, size, width = plan[i]
        columns = pl.ds(pl.multiple_of(section * width, 128), width)
        source = inputs[index].at[pl.ds(start, size), columns]
        there = unit(i, 1 if up else stacks - 1)
        return remote(
            source, block(i, stack, core, section), next_send.at[i, int(up)], stack_recv.at[there], beyond(up)
        )

    def pass_copy(i, k, up):
        here = block(i, from_stack_of(k), core, section)
        there = unit(i, k + 1 if up else k - 1)
        return remote(here, here, pass_send.at[unit(i, k)], stack_recv.at[there], beyond(up))

    def arrival(i, k):
        here = block(i, from_stack_of(k), core, section)
        return remote(here, here, pass_send.at[unit(i, k)], stack_recv.at[unit(i, k)], sibling)

    def goes(k, up):
        if up:
            return (stack >= k) & (stack < stacks - 1)
        return (stack < k) & (stack > 0)

    def pair_copy(u, which, arrived):
        i, k = units[u]
        first, second = (over_x, over_y) if u % 2 == 0 else (over_y, over_x)
        owner = from_stack_of(k)
        here = block(i, owner, core, (section, section, first)[which])
        came = block(i, owner, core, (first, second, 3 - section)[which])
        device = (first if which == 0 else second, member)
        return remote(
            here, came if arrived else here, pair_send.at[u, which], pair_recv.at[u, which], device
        )

    def core_copy(u, arrived):
        i, k = units[u]
        here = block(i, from_stack_of(k), core, None)
        came = block(i, from_stack_of(k), 1 - core, None)
        return remote(here, came if arrived else here, core_send.at[u], core_recv.at[u], sibling)

    def own_copy(m, arrived):
        target = outs[m].at[member + 1 - 2 * core] if arrived else outs[m].at[member]
        return remote(inputs[m], target, own_send.at[m], own_recv.at[m], sibling)

    def swap_copy(j, k, arrived):
        target = lax.rem(member + members - k - 1, members) if arrived else member
        return remote(
            inputs[matrices + j].at[lax.rem(member + k + 1, members)],
            outs[matrices + j].at[target],
            swap_send.at[j, k],
            swap_recv.at[j, k],
            line[k],
        )

    kept = [pltpu.make_async_copy(inputs[m], outs[m].at[member], keep.at[m]) for m in range(matrices)]
    kept += [
        pltpu.make_async_copy(inputs[j].at[member], outs[j].at[member], keep.at[j])
        for j in range(matrices, count)
    ]

    def both_ways(chosen, act):
        for i in chosen:
            for up in (True, False):

                @pl.when((stack < stacks - 1) if up else (stack > 0))
                def _():
                    act(next_copy(i, up))

    ahead = 2
    both_ways(range(min(ahead, pieces)), lambda copy: copy.start())
    for copy in kept:
        copy.start()

    def passing(u, act):
        i, k = units[u]
        for up in (True, False):

            @pl.when(goes(k, up))
            def _():
                act(pass_copy(i, k, up))

    def from_stack(u):
        arrival(*units[u]).wait_recv()
        passing(u, lambda copy: copy.start())
        pair_copy(u, 0, False).start()

    def from_first(u):
        pair_copy(u, 0, True).wait_recv()
        for which in (1, 2):
            pair_copy(u, which, False).start()

    def from_second(u):
        for which in (1, 2):
            pair_copy(u, which, True).wait_recv()
        core_copy(u, False).start()

    lag = 3
    for step in range(len(units) + 2 * lag):
        chunk, turn = divmod(step, stacks - 1)
        if turn == 0 and chunk + ahead < pieces:
            both_ways([chunk + ahead], lambda copy: copy.start())
        if turn == 1 and 1 <= chunk <= matrices:
            own_copy(chunk - 1, False).start()
        if turn == 2 and chunk < members - 1:
            for j in range(swaps):
                swap_copy(j, chunk, False).start()
        for depth, stage in enumerate((from_stack, from_first, from_second)):
            if 0 <= step - lag * depth < len(units):
                stage(step - lag * depth)
    both_ways(range(pieces), lambda copy: copy.wait_send())
    for u in range(len(units)):
        passing(u, lambda copy: copy.wait_send())
        for which in range(3):
            pair_copy(u, which, False).wait_send()
        core_copy(u, False).wait_send()
        core_copy(u, True).wait_recv()
    for m in range(matrices):
        own_copy(m, False).wait_send()
        own_copy(m, True).wait_recv()
    for copy in kept:
        copy.wait()
    for j in range(swaps):
        for k in range(members - 1):
            swap_copy(j, k, False).wait_send()
            swap_copy(j, k, True).wait_recv()


def gather_kernel(matrices, swaps, members, collective_id):
    plan = []
    for index, part in enumerate(matrices):
        rows, cols = part.shape
        size = max(size for size in range(16, rows + 1, 16) if rows % size == 0 and size * cols <= 340000)
        plan += [(index, start, size, cols // 4) for start in range(0, rows, size)]
    units = len(plan) * (members // 2 - 1)
    dma = pltpu.SemaphoreType.DMA
    count = len(swaps)
    return pl.pallas_call(
        functools.partial(gather_body, members, plan, (len(matrices), count)),
        out_shape=[jax.ShapeDtypeStruct((members,) + part.shape, bf16) for part in matrices]
        + [jax.ShapeDtypeStruct(part.shape, bf16) for part in swaps],
        in_specs=in_place(len(matrices) + count),
        out_specs=in_place(len(matrices) + count),
        scratch_shapes=[
            dma((len(plan), 2)),
            dma((units,)),
            dma((units,)),
            dma((units, 3)),
            dma((units, 3)),
            dma((units,)),
            dma((units,)),
            dma((len(matrices),)),
            dma((len(matrices),)),
            dma((len(matrices) + count,)),
            dma((count, members - 1)),
            dma((count, members - 1)),
        ],
        compiler_params=pltpu.CompilerParams(collective_id=collective_id, has_side_effects=True),
        name="gather_rows",
    )(*matrices, *swaps)


def find_body(members, asked, counts, table, main_ref, tail_ref, main, tail, main_found, tail_found):
    capacity = main_ref.shape[1]
    part = capacity // 4
    step = 512

    @pl.loop(0, table.shape[1] // step)
    def _(i):
        start = pl.multiple_of(i * step, step)
        block = table[:, pl.ds(start, step)]
        main[pl.ds(start, step), :] = block[:MAIN].T
        tail[pl.ds(start, step), :] = block[MAIN:].T

    @pl.loop(0, members)
    def _(k):
        first = pl.multiple_of(k * capacity, 16)

        @pl.loop(0, (counts[k] + 7) // 8)
        def _(i):
            base = pl.multiple_of(first + i * 8, 8)
            for u in range(8):
                there = pl.ds(asked[base + u], 1)
                main_found[pl.ds(base + u, 1), :] = main[there, :]
                tail_found[pl.ds(base + u, 1), :] = tail[there, :]

        main_ref[k] = main_found[pl.ds(first, capacity), :].astype(bf16)
        pieces = [tail_found[pl.ds(first + j * part, part), :] for j in range(4)]
        tail_ref[k] = jnp.concatenate(pieces, axis=1).astype(bf16)


def find_rows(table, asked, counts, members, capacity):
    rows = table.shape[0]
    shape = jax.ShapeDtypeStruct
    smem = pl.BlockSpec(memory_space=pltpu.SMEM)
    return pl.pallas_call(
        functools.partial(find_body, members),
        out_shape=[shape((members, capacity, MAIN), bf16), shape((members, capacity // 4, MAIN), bf16)],
        in_specs=[smem, smem] + whole(1),
        out_specs=whole(2),
        scratch_shapes=[
            pltpu.VMEM((rows, MAIN), f32),
            pltpu.VMEM((rows, TAIL), f32),
            pltpu.VMEM((members * capacity, MAIN), f32),
            pltpu.VMEM((members * capacity, TAIL), f32),
        ],
        compiler_params=kernel_params(),
        name="find_rows",
    )(asked, counts, table.T)


def unpack_body(slots, main_ref, tail_ref, rows_ref, main, tail, main_row, tail_row):
    members, capacity, _ = main_ref.shape
    part = capacity // 4

    @pl.loop(0, members)
    def _(k):
        start = pl.multiple_of(k * capacity, 16)
        main[pl.ds(start, capacity), :] = main_ref[k].astype(f32)
        wide = tail_ref[k].astype(f32)
        for j in range(4):
            tail[pl.ds(start + j * part, part), :] = wide[:, j * TAIL : (j + 1) * TAIL]

    @pl.loop(0, rows_ref.shape[0] // 16)
    def _(i):
        start = pl.multiple_of(i * 16, 16)
        for u in range(16):
            slot = pl.ds(slots[start + u], 1)
            main_row[pl.ds(start + u, 1), :] = main[slot, :]
            tail_row[pl.ds(start + u, 1), :] = tail[slot, :]

    @pl.loop(0, rows_ref.shape[0] // 32)
    def _(i):
        where = pl.ds(pl.multiple_of(i * 32, 32), 32)
        rows_ref[where, :] = jnp.concatenate([main_row[where, :], tail_row[where, :]], axis=1).astype(bf16)


def unpack_rows(main, tail, slots):
    count = slots.shape[0]
    members, capacity, _ = main.shape
    return pl.pallas_call(
        unpack_body,
        out_shape=jax.ShapeDtypeStruct((count, D), bf16),
        in_specs=[pl.BlockSpec(memory_space=pltpu.SMEM)] + whole(2),
        out_specs=pl.BlockSpec(memory_space=pltpu.VMEM),
        scratch_shapes=[
            pltpu.VMEM((members * capacity, MAIN), f32),
            pltpu.VMEM((members * capacity, TAIL), f32),
            pltpu.VMEM((count, MAIN), f32),
            pltpu.VMEM((count, TAIL), f32),
        ],
        compiler_params=kernel_params(),
        name="unpack_rows",
    )(slots, main, tail)


def table_body(quarter, main_ref, tail_ref, table, first, second, table_out, first_out, second_out, tail):
    tail[...] = tail_ref[...].astype(f32).T
    start = pl.multiple_of(pl.program_id(0) // quarter * TAIL, TAIL)
    grad = jnp.concatenate([main_ref[...].astype(f32).T, tail[pl.ds(start, TAIL), :]], axis=0)
    stepped = adam_step(table[...], grad, first[...], second[...], 1.0, 0.0)
    table_out[...], first_out[...], second_out[...] = stepped


def table_step(main, tail, table, first, second):
    rows = table.shape[0]
    tile = 512
    quarter = rows // 4 // tile
    wide = pl.BlockSpec((D, tile), lambda i: (0, i))
    stepped = pl.pallas_call(
        functools.partial(table_body, quarter),
        grid=(rows // tile,),
        out_shape=[jax.ShapeDtypeStruct((D, rows), f32)] * 3,
        in_specs=[
            pl.BlockSpec((tile, MAIN), lambda i: (i, 0)),
            pl.BlockSpec((tile, MAIN), lambda i: (i % quarter, 0)),
        ]
        + [wide] * 3,
        out_specs=[wide] * 3,
        scratch_shapes=[pltpu.VMEM((MAIN, tile), f32)],
        compiler_params=kernel_params(),
        name="table_step",
    )(main, tail, table.T, first.T, second.T)
    return [part.T for part in stepped]


def place_numbers(numbers, slots, count):
    high = (slots[:, None] // 128 == jnp.arange(count // 128)[None, :]).astype(bf16)
    low = (slots[:, None] % 128 == jnp.arange(128)[None, :]).astype(bf16)
    upper, lower = (numbers // 64).astype(bf16), (numbers % 64).astype(bf16)
    placed = 64.0 * jnp.einsum("rh,rl->hl", high, low * upper[:, None], preferred_element_type=f32)
    placed += jnp.einsum("rh,rl->hl", high, low * lower[:, None], preferred_element_type=f32)
    return placed.astype(jnp.int32).reshape(-1)


def reduce_plain(grads, members):
    totals = []
    for grad in grads:
        part = lax.psum_scatter(grad, ("dp", "section"), scatter_dimension=0, tiled=True)
        totals.append(lax.all_gather(part, "section", axis=0, tiled=True))
    return totals


def per_device(
    ids,
    masks,
    labels,
    table,
    table_first,
    table_second,
    null_tokens,
    null_first,
    null_second,
    w_up,
    up_first,
    up_second,
    w_down,
    down_first,
    down_second,
    w_top,
    top_first,
    top_second,
    gains,
    gains_first,
    gains_second,
    biases,
    biases_first,
    biases_second,
    mixers,
    mixers_first,
    mixers_second,
    top_bias,
    top_bias_first,
    top_bias_second,
    head,
    head_first,
    head_second,
):
    sections = lax.axis_size("section")
    members = lax.axis_size("dp")
    section_index = lax.axis_index("section")
    micro_count = masks.shape[0]
    batch_rows = masks.shape[1]
    total = micro_count * batch_rows * members

    flat_ids = ids[0].T.reshape(-1)
    id_count = flat_ids.shape[0]
    capacity = 2 * id_count // members
    rows_dev = table.shape[0]
    owners = flat_ids // rows_dev
    local_rows = flat_ids - owners * rows_dev
    hits = (owners[:, None] == jnp.arange(members, dtype=jnp.int32)[None, :]).astype(jnp.int32)
    ranks = jnp.sum(jnp.cumsum(hits, axis=0) * hits, axis=1) - 1
    slots = owners * capacity + ranks
    requests = place_numbers(local_rows + 1, slots, members * capacity)
    asked = lax.all_to_all(
        requests.reshape(members, capacity), "dp", split_axis=0, concat_axis=0, tiled=True
    )
    asked_counts = jnp.sum((asked > 0).astype(jnp.int32), axis=1)
    asked = jnp.maximum(asked.reshape(-1) - 1, 0)
    kernels_fit = members == 8 and sections == 4
    if kernels_fit:
        main, tail = find_rows(table, asked, asked_counts, members, capacity)
        matrices = [w.astype(bf16).reshape(-1, w.shape[-1]) for w in (w_up, w_down, w_top)]
        up_copies, down_copies, top_copy, main, tail = gather_kernel(matrices, [main, tail], members, 2)
        top_copy = top_copy.reshape(-1, TOP_HID)
        looked = unpack_rows(main, tail, slots)
    else:
        found = jnp.take(table.astype(bf16), asked, axis=0, mode="clip")
        fetched = lax.all_to_all(
            found.reshape(members, capacity, D), "dp", split_axis=0, concat_axis=0, tiled=True
        ).reshape(members * capacity, D)
        looked = jnp.take(fetched, slots, axis=0, mode="clip")
        up_copies = gather_rows(w_up, section_index, sections, 1)[:, None]
        down_copies = gather_rows(w_down, section_index, sections, 1)[:, None]
        top_copy = gather_rows(w_top, section_index, sections, 0)
    looked = looked.reshape(FEATS, batch_rows, D)

    present = lax.dynamic_index_in_dim(masks, section_index, 0, keepdims=False).T > 0
    targets = lax.dynamic_index_in_dim(labels, section_index, 0, keepdims=False).astype(f32)
    state = jnp.where(present[..., None], looked, null_tokens.astype(bf16)[:, None, :])
    values = [layer_values(gains[depth], biases[depth], mixers[depth]) for depth in range(2)]
    states, kept = [], []
    for depth in range(2):
        states.append(state)
        state, *stored = layer_forward(depth, state, up_copies, down_copies, values[depth])
        kept.append(stored)
    losses, upstream, grad_top, grad_top_bias, grad_head = top_pass(
        state, top_copy, top_bias, head, targets, total
    )
    losses = losses[None, :]
    layer_grads = [None, None]
    for depth in (1, 0):
        upstream, *layer_grads[depth] = layer_backward(
            depth, upstream, states[depth], kept[depth], up_copies, down_copies, values[depth]
        )
    grad_looked = jnp.where(present[..., None], upstream, jnp.zeros_like(upstream))
    grad_null = jnp.sum(jnp.where(present[..., None], 0.0, upstream.astype(f32)), axis=1)
    input_grad = grad_looked.transpose(1, 0, 2)[None]
    smalls = (
        grad_null,
        jnp.stack([layer_grads[0][2], layer_grads[1][2]]),
        jnp.stack([layer_grads[0][3], layer_grads[1][3]]),
        jnp.stack([layer_grads[0][4], layer_grads[1][4]]),
        grad_top_bias[None, :],
        grad_head[None, :],
    )
    matrix_pairs = [pair for depth in range(2) for pair in layer_grads[depth][:2]]
    if kernels_fit:
        main, tail = pack_rows(grad_looked.reshape(id_count, D), slots, members, capacity)
        top_grad, *totals = reduce_kernel(
            [grad_top] + matrix_pairs, [], [main, tail], smalls, members, 0
        )
        matrix_grads, (main, tail), small_total = totals[:4], totals[4:6], totals[6:]
        main, tail = add_rows(main, tail, asked, asked_counts, rows_dev)
        main, tail = reduce_kernel([], [main, tail], [], [], members, 1)
        table_out = table_step(main, tail, table, table_first, table_second)
    else:
        outgoing = (
            jnp.zeros((members * capacity, D), bf16)
            .at[slots]
            .set(grad_looked.reshape(id_count, D), unique_indices=True, mode="promise_in_bounds")
        )
        arrived_rows = lax.all_to_all(
            outgoing.reshape(members, capacity, D), "dp", split_axis=0, concat_axis=0, tiled=True
        ).reshape(members * capacity, D)
        table_part = jnp.zeros((rows_dev, D), f32).at[asked].add(arrived_rows.astype(f32))
        table_sum = lax.psum_scatter(
            table_part.astype(bf16), "section", scatter_dimension=0, tiled=True
        )
        table_grad = lax.all_gather(table_sum, "section", axis=0, tiled=True).astype(f32)
        table_out = adam_step(table, table_grad, table_first, table_second, 1.0, 0.0)
        top_grad, *matrix_grads = reduce_plain(
            [nn(left, right).astype(bf16) for left, right in [grad_top] + matrix_pairs], members
        )
        small_total = lax.psum(smalls, ("section", "dp"))
    top_grad = top_grad.astype(f32)
    up_grad = jnp.stack([matrix_grads[0], matrix_grads[2]]).astype(f32)
    down_grad = jnp.stack([matrix_grads[1], matrix_grads[3]]).astype(f32)
    null_out = adam_step(null_tokens, small_total[0], null_first, null_second, 1.0, 0.0)
    up_out = adam_step(w_up, up_grad, up_first, up_second, 0.05, 0.01)
    down_out = adam_step(w_down, down_grad, down_first, down_second, 0.05, 0.01)
    top_out = adam_step(w_top, top_grad, top_first, top_second, 0.05, 0.01)
    gains_out = adam_step(gains, small_total[1], gains_first, gains_second, 1.0, 0.0)
    biases_out = adam_step(biases, small_total[2], biases_first, biases_second, 0.1, 0.0)
    mixers_out = adam_step(mixers, small_total[3], mixers_first, mixers_second, 0.2, 0.01)
    top_bias_out = adam_step(top_bias, small_total[4][0], top_bias_first, top_bias_second, 0.1, 0.0)
    head_out = adam_step(head, small_total[5][0], head_first, head_second, 0.1, 0.0)
    return (
        losses,
        input_grad,
        table_out[0],
        table_out[1],
        table_out[2],
        null_out[0],
        null_out[1],
        null_out[2],
        up_out[0],
        up_out[1],
        up_out[2],
        down_out[0],
        down_out[1],
        down_out[2],
        top_out[0],
        top_out[1],
        top_out[2],
        gains_out[0],
        gains_out[1],
        gains_out[2],
        biases_out[0],
        biases_out[1],
        biases_out[2],
        mixers_out[0],
        mixers_out[1],
        mixers_out[2],
        top_bias_out[0],
        top_bias_out[1],
        top_bias_out[2],
        head_out[0],
        head_out[1],
        head_out[2],
    )


def solution(mesh):
    placed = (
        P("section", "dp", None),
        P(None, "dp", None),
        P(None, "dp"),
        P("dp", None),
        P("dp", None),
        P("dp", None),
        P(),
        P(),
        P(),
        P(None, "dp", None),
        P(None, "dp", None),
        P(None, "dp", None),
        P(None, "dp", None),
        P(None, "dp", None),
        P(None, "dp", None),
        P("dp", None),
        P("dp", None),
        P("dp", None),
        P(),
        P(),
        P(),
        P(),
        P(),
        P(),
        P(),
        P(),
        P(),
        P(),
        P(),
        P(),
        P(),
        P(),
        P(),
    )
    return jax.shard_map(
        per_device,
        mesh=mesh,
        in_specs=placed,
        out_specs=(
            P("section", "dp"),
            P("section", "dp", None, None),
            P("dp", None),
            P("dp", None),
            P("dp", None),
            P(),
            P(),
            P(),
            P(None, "dp", None),
            P(None, "dp", None),
            P(None, "dp", None),
            P(None, "dp", None),
            P(None, "dp", None),
            P(None, "dp", None),
            P("dp", None),
            P("dp", None),
            P("dp", None),
            P(),
            P(),
            P(),
            P(),
            P(),
            P(),
            P(),
            P(),
            P(),
            P(),
            P(),
            P(),
            P(),
            P(),
            P(),
        ),
        check_vma=False,
    )
```

time: 4620 us -> 768 us (0.17)
  waiting for transfers between devices: 2390 us -> 0.01 us
  blocking collectives: 986 us -> 0 us
  Pallas kernels: 0 us -> 670 us
  local copies, waits for them, and re-layouts: 460 us -> 14.9 us
  loops' own time: 270 us -> 0 us
  starting transfers between devices: 249 us -> 6.53 us
  other arithmetic: 228 us -> 54.9 us
    ppermute x12 -> x0, waiting for transfers between devices: 1800 us -> none  [shifted(): return lax.ppermute(value, axis, pairs)]
    unnamed x1 -> x0, blocking collectives: 859 us -> none
    pallas_call x0 -> x13, Pallas kernels: none -> 670 us  [the longest x2 284 us: reduce_kernel(): pl.pallas_call(functools.partial(reduce_body, plan, slots, (count, len(pl...]
    all_gather x3 -> x0, waiting for transfers between devices: 476 us -> none  [the longest x1 188 us: per_device(): lax.all_gather(for_sending(own_pack), 'dp', axis=0, tiled=True)]
    another operation x15 -> x0, loops' own time: 270 us -> none  [the longest x7 168 us: per_device(): lax.switch(chosen, backwards, stored, upstream, which_micro, packed_sum,...]
    ppermute x12 -> x0, starting transfers between devices: 216 us -> none  [shifted(): return lax.ppermute(value, axis, pairs)]
    gather x3 -> x0, local copies, waits for them, and re-layouts: 138 us -> none  [the longest x1 89.8 us: per_device(): looked = fetched[owners, slots].reshape(1, batch_rows, FEATS, D)]
    all_to_all x2 -> x0, blocking collectives: 127 us -> none  [the longest x1 79.3 us: per_device(): lax.all_to_all(found, 'dp', split_axis=0, concat_axis=0, tiled=True)]
  transfers between devices with their start and end apart: 20 -> 1, of which waited for: 17 -> 0; matrix products, arithmetic and copies ran while one was open for 4% -> 2% of each run, Pallas kernels for 0% -> 0%
where the time goes in v1:
time: 768 us; the launch traced here: 754 us
  Pallas kernels  670 us (87%)
  other arithmetic  54.9 us (7%)
  local copies, waits for them, and re-layouts  14.9 us (2%)
    pallas_call x2, Pallas kernels, reduce_kernel(): pl.pallas_call(functools.partial(reduce_body, plan, slots, (count, len(pl...  284 us
    pallas_call x1, Pallas kernels, gather_kernel(): pl.pallas_call(functools.partial(gather_body, members, plan, (len(matrice...  182 us
    pallas_call x2, Pallas kernels, layer_backward(): pl.pallas_call(functools.partial(backward_body, depth), out_shape=[shape(...  64.9 us
    pallas_call x2, Pallas kernels, layer_forward(): pl.pallas_call(functools.partial(forward_body, depth), out_shape=[shape((...  41.4 us
    sub x9, other arithmetic, adam_step(): values - rate * (first_hat / (jnp.sqrt(second_hat) + adam_eps) + decay *...  25.3 us
    pallas_call x1, Pallas kernels, top_pass(): pl.pallas_call(lambda *refs: top_body(*refs[:5], float(total), *refs[5:])...  21.6 us
    pallas_call x1, Pallas kernels, add_rows(): pl.pallas_call(functools.partial(add_body, members), out_shape=[shape((ro...  20.2 us
  transfers between devices with their start and end apart: 1, of which 0 were waited for; matrix products, arithmetic and copies ran while one was open for 2% of the time, Pallas kernels for 0%

profile of v1, /device:TPU:0, one launch (start us, length us, event | category | flops | bytes accessed | tf_op | source)
XLA Modules:
  0.0 754.0 jit_solution(13636242956377446214)
XLA Ops:
  0.7 0.8 broadcast_divide_fusion
  1.4 0.8 fusion.37
  2.5 2.3 reduce-window.6
  4.8 0.3 slice_reduce_fusion
  5.1 0.2 reduce-window.9
  5.3 0.1 add_bitcast_fusion
  5.4 0.8 reshape.435
  6.5 3.0 fusion.16
  9.5 3.6 fusion.22
  13.1 6.5 all-to-all-start
  19.6 0.6 fusion.70
  20.2 0.6 fusion.67
  20.9 0.6 fusion.68
  21.5 0.6 fusion.69
  22.1 4.5 convert_element_type.132.refs_2_
  26.6 1.5 convert_element_type.131
  28.1 0.1 copy-done.3
  28.2 0.9 convert_element_type.130
  29.3 0.4 multiply_convert_fusion
  29.7 1.4 convert_element_type.143.compress
  31.2 0.6 broadcast_bitcast_fusion.1.projector
  31.9 1.4 convert_element_type.148.compress
  33.4 0.6 broadcast_bitcast_fusion.projector
  34.0 0.8 fusion.36
  34.8 0.8 copy.77.refs_4_
  35.6 0.6 broadcast_in_dim.55.refs_3_
  36.2 0.7 copy.78
  36.9 0.7 copy.79
  37.6 1.3 fusion.34
  38.9 15.2 %find_rows.1 = (bf16[8,1280,128]{2,1,0:T(8,128)(2,1)}, bf16[8,320,128]{2,1,0:T(8,128)(2,1)}) custom-call(s32[10240]{0:T(1024)} %bitcast.88, s32[8]{0:T(128)} %get-tuple-element.289.counts, f32[160,6144]{1,0:T(8,128)} %bitcast.71), custom_call_target="tpu_custom_call" | custom-call | tf_op jit(solution)/shard_map/find_rows/pallas_call | solution.py:1165
  54.1 182.2 %gather_rows.1 = (bf16[8,192,1536]{2,1,0:T(8,128)(2,1)}, bf16[8,384,2560]{2,1,0:T(8,128)(2,1)}, bf16[8,640,2048]{2,1,0:T(8,128)(2,1)}, bf16[8,1280,128]{2,1,0:T(8,128)(2,1)}, bf16[8,320,128]{2,1,0:T(8,128)(2,1)}) custom-call(bf16[192,1536]{1,0:T(8,128)(2,1)} %bitcast.79, bf16[384,2560]{1,0:T(8,128)(2,1)} %bitcast.75, ...), custom_call_target="tpu_custom_call" | custom-call | tf_op jit(solution)/shard_map/gather_rows/pallas_call | solution.py:1107
  236.3 13.1 %unpack_rows.1 = bf16[5120,160]{1,0:T(8,128)(2,1)} custom-call(s32[5120]{0:T(1024)} %copy-done.12, bf16[8,1280,128]{2,1,0:T(8,128)(2,1)} %get-tuple-element.93.main_ref, bf16[8,320,128]{2,1,0:T(8,128)(2,1)} %get-tuple-element.94.tail_ref), custom_call_target="tpu_custom_call" | custom-call | tf_op jit(solution)/shard_map/unpack_rows/pallas_call | solution.py:1210
  249.4 4.4 broadcast_select_fusion.1.x_ref
  253.9 20.7 %layer_forward.2 = (bf16[32,160,160]{2,1,0:T(8,128)(2,1)}, f32[32,160,160]{2,1,0:T(8,128)}, f32[160,768]{1,0:T(8,128)}, bf16[768,160]{1,0:T(8,128)(2,1)}, f32[16...) custom-call(bf16[32,160,160]{2,1,0:T(8,128)(2,1)} %broadcast_select_fusion.1.x_ref, ...), custom_call_target="tpu_custom_call" | custom-call | tf_op jit(solution)/shard_map/layer_forward/pallas_call | solution.py:345
  274.6 20.7 %layer_forward.3 = (bf16[32,160,160]{2,1,0:T(8,128)(2,1)}, f32[32,160,160]{2,1,0:T(8,128)}, f32[160,768]{1,0:T(8,128)}, bf16[768,160]{1,0:T(8,128)(2,1)}, f32[16...) custom-call(bf16[32,160,160]{2,1,0:T(8,128)(2,1)} %get-tuple-element.97.x_ref, bf16[8,192,1536]{2,1,0:T(8,128)(2,1)} %get-tuple-element.95.up_hbm, ...), custom_call_target="tpu_custom_call" | custom-call | tf_op jit(solution)/shard_map/layer_forward/pallas_call | solution.py:345
  295.3 21.6 %top_pass.1 = (bf16[5120,160]{1,0:T(8,128)(2,1)}, f32[160,1]{1,0:T(8,128)}, bf16[160,2048]{1,0:T(8,128)(2,1)}, bf16[32,160,160]{2,1,0:T(8,128)(2,1)}, f32[1,2048]{1,0:T(1,128)}, /*index=5*/f32[1,2048]{1,0:T(1,128)}) custom-call(bf16[32,160,160]{2,1,0:T(8,128)(2,1)} %get-tuple-element.98.refs_0_, bf16[5120,2048]{1,0:T(8,128)(2,1)} %bitcast.70, ...), custom_call_target="tpu_custom_call" | custom-call | tf_op jit(solution)/shard_map/top_pass/pallas_call | solution.py:423
  316.9 32.5 %layer_backward.2 = (bf16[32,160,160]{2,1,0:T(8,128)(2,1)}, bf16[160,2560]{1,0:T(8,128)(2,1)}, bf16[160,1536]{1,0:T(8,128)(2,1)}, f32[1,928]{1,0:T(1,128)}, f32[1,5024]{1,0:T(1,128)}, /*index=5*/f32[1,1280]{1,0:T(1,128)}) custom-call(bf16[32,160,160]{2,1,0:T(8,128)(2,1)} %get-tuple-element.101.upstream, bf16[32,160,160]{2,1,0:T(8,128)(2,1)} %get-tuple-element.97.x_ref, ...), custom_call_target="tpu_custom_call" | custom-call | tf_op jit(solution)/shard_map/layer_backward/pallas_call | solution.py:379
  349.4 32.5 %layer_backward.3 = (bf16[32,160,160]{2,1,0:T(8,128)(2,1)}, bf16[160,2560]{1,0:T(8,128)(2,1)}, bf16[160,1536]{1,0:T(8,128)(2,1)}, f32[1,928]{1,0:T(1,128)}, f32[1,5024]{1,0:T(1,128)}, /*index=5*/f32[1,1280]{1,0:T(1,128)}) custom-call(bf16[32,160,160]{2,1,0:T(8,128)(2,1)} %get-tuple-element.105.upstream, bf16[32,160,160]{2,1,0:T(8,128)(2,1)} %broadcast_select_fusion.1.x_ref, ...), custom_call_target="tpu_custom_call" | custom-call | tf_op jit(solution)/shard_map/layer_backward/pallas_call | solution.py:379
  381.9 4.6 broadcast_select_fusion
  386.5 1.8 select_reduce_fusion.refs_12_
  388.3 1.0 fusion.73
  389.3 0.2 fusion.32
  389.5 0.6 multiply_reduce_fusion
  390.1 0.6 pad_maximum_fusion.3
  390.7 0.6 broadcast_in_dim.98.refs_17_
  391.3 11.9 %pack_rows.1 = (bf16[8,1280,128]{2,1,0:T(8,128)(2,1)}, bf16[8,320,128]{2,1,0:T(8,128)(2,1)}) custom-call(s32[5120]{0:T(1024)} %copy-done.12, bf16[5120,160]{1,0:T(8,128)(2,1)} %bitcast.73), custom_call_target="tpu_custom_call" | custom-call | tf_op jit(solution)/shard_map/pack_rows/pallas_call | solution.py:853
  403.3 3.0 copy.80
  406.2 0.6 fusion.52
  406.8 0.6 pad_maximum_fusion.4.refs_15_
  407.5 0.7 pad_maximum_fusion.2.refs_14_
  408.1 0.6 pad_maximum_fusion.5.refs_13_
  408.7 244.8 %reduce_rows.2 = (bf16[640,2048]{1,0:T(8,128)(2,1)}, bf16[96,1536]{1,0:T(8,128)(2,1)}, bf16[192,2560]{1,0:T(8,128)(2,1)}, bf16[96,1536]{1,0:T(8,128)(2,1)}, bf16...) custom-call(bf16[4,2,640,160]{3,2,1,0:T(8,128)(2,1)} %bitcast.78, ...), custom_call_target="tpu_custom_call" | custom-call | tf_op jit(solution)/shard_map/reduce_rows/pallas_call | solution.py:783
  653.6 20.2 %add_rows.1 = (bf16[6144,128]{1,0:T(8,128)(2,1)}, bf16[1536,128]{1,0:T(8,128)(2,1)}) custom-call(s32[10240]{0:T(1024)} %bitcast.89, s32[8]{0:T(128)} %get-tuple-element.289.counts, bf16[8,1280,128]{2,1,0:T(8,128)(2,1)} %get-tuple-element.130.main_ref, bf16[8,320,128]{2,1,0:T(8,128)(2,1)} %get-tuple-element.131.tail_ref), custom_call_target="tpu_custom_call" | custom-call | tf_op jit(solution)/shard_map/add_rows/pallas_call | solution.py:906
  673.8 39.5 %reduce_rows.3 = (bf16[6144,128]{1,0:T(8,128)(2,1)}, bf16[1536,128]{1,0:T(8,128)(2,1)}) custom-call(bf16[4,1536,128]{2,1,0:T(8,128)(2,1)} %bitcast.80, bf16[4,384,128]{2,1,0:T(8,128)(2,1)} %bitcast.87), custom_call_target="tpu_custom_call" | custom-call | tf_op jit(solution)/shard_map/reduce_rows/pallas_call | solution.py:783
  713.6 12.9 %multiply_subtract_fusion = (f32[640,2048]{1,0:T(8,128)}, f32[640,2048]{1,0:T(8,128)}, f32[640,2048]{1,0:T(8,128)}) fusion(f32[640,2048]{1,0:T(8,128)} %param.48, bf16[640,2048]{1,0:T(8,128)(2,1)} %get-tuple-element.144, f32[640,2048]{1,0:T(8,128)} %param.49, f32[640,2048]{1,0:T(8,128)} %param.50), kind=kLoop, calls=%fused_computation.5 | loop fusion | flops 20971520 | bytes 34078720 | tf_op jit(solution)/shard_map/sub | solution.py:42
  726.5 0.8 multiply_subtract_fusion.3
  727.3 0.7 add_subtract_fusion
  727.9 0.6 multiply_subtract_fusion.4
  728.6 0.6 multiply_subtract_fusion.5
  729.3 0.6 multiply_subtract_fusion.6
  729.9 0.6 add_subtract_fusion.1
  730.6 6.0 multiply_subtract_fusion.1
  736.6 2.4 multiply_subtract_fusion.2
  739.0 14.8 %table_step.1 = (f32[160,6144]{1,0:T(8,128)}, f32[160,6144]{1,0:T(8,128)}, f32[160,6144]{1,0:T(8,128)}) custom-call(bf16[6144,128]{1,0:T(8,128)(2,1)} %get-tuple-element.134.main_ref, bf16[1536,128]{1,0:T(8,128)(2,1)} %get-tuple-element.135.tail_ref, f32[160,6144]{1,0:T(8,128)} %bitcast.72, f32[160,6144]{1,0:T(8,128)} %bitcast.76, f32[160,6144]{1,0:T(8,128)} %bitcast.77), custom_call_target="tpu_custom_call" | custom-call | tf_op jit(solution)/shard_map/table_step/pallas_call | solution.py:1239
  (116 shorter events, 1.0 us)
Async XLA Ops:
  6.4 6.6 copy-start.12
  6.5 13.1 %copy-start.15 = (f32[2,5024]{1,0:T(2,128)S(1)}, f32[2,5024]{1,0:T(2,128)}, u32[]{:S(2)}) copy-start(f32[2,5024]{1,0:T(2,128)} %param.54) | copy-start | bytes 120580
  6.5 13.1 %copy-start.27 = (f32[2,928]{1,0:T(2,128)S(1)}, f32[2,928]{1,0:T(2,128)}, u32[]{:S(2)}) copy-start(f32[2,928]{1,0:T(2,128)} %param.51) | copy-start | bytes 22276
  9.5 11.3 %copy-start.22 = (f32[2,1280]{1,0:T(2,128)S(1)}, f32[2,1280]{1,0:T(2,128)}, u32[]{:S(2)}) copy-start(f32[2,1280]{1,0:T(2,128)} %param.57) | copy-start | bytes 30724
  13.1 24.5 %all-to-all-start = ((s32[8,1,1280]{2,1,0:T(1,128)}), s32[8,1,1280]{2,1,0:T(1,128)S(1)}, u32[]{:S(2)}, u32[]{:S(2)}) async-start(s32[8,1,1280]{2,1,0:T(1,128)} %bitcast.8), calls=%async_computation | async-start | bytes 81920 | tf_op jit(solution)/shard_map/all_to_all | solution.py:1325
  22.1 4.5 copy-start.1
  26.6 1.6 copy-start.3
  26.6 2.5 copy-start.16
  29.1 5.7 copy-start.47
  29.1 6.4 copy-start.18
  31.1 23.0 %copy-start.8 = (bf16[128,256]{1,0:T(8,128)(2,1)}, bf16[128,256]{1,0:T(8,128)(2,1)S(1)}, u32[]{:S(2)}) copy-start(bf16[128,256]{1,0:T(8,128)(2,1)S(1)} %convert_element_type.143.compress) | copy-start | bytes 196612
  33.3 203.0 %copy-start.9 = (bf16[128,256]{1,0:T(8,128)(2,1)}, bf16[128,256]{1,0:T(8,128)(2,1)S(1)}, u32[]{:S(2)}) copy-start(bf16[128,256]{1,0:T(8,128)(2,1)S(1)} %convert_element_type.148.compress) | copy-start | bytes 196612
  381.9 4.6 copy-start
  388.3 1.0 copy-start.17
  388.3 1.8 copy-start.42
  403.2 3.6 copy-start.43
  403.2 3.6 copy-start.44
  403.2 4.2 copy-start.28
  403.2 4.2 copy-start.29
  403.3 4.9 copy-start.45
  403.3 4.8 copy-start.46
  653.6 59.7 %copy-start.35 = (f32[1,2049]{1,0:T(1,128)S(1)}, f32[1,2049]{1,0:T(1,128)}, u32[]{:S(2)}) copy-start(f32[1,2049]{1,0:T(1,128)} %get-tuple-element.149) | copy-start | bytes 24592
  713.3 13.1 %copy-start.19 = (f32[2,5024]{1,0:T(2,128)S(1)}, f32[2,5024]{1,0:T(2,128)}, u32[]{:S(2)}) copy-start(f32[2,5024]{1,0:T(2,128)} %param.55) | copy-start | bytes 120580
  713.4 13.1 %copy-start.20 = (f32[2,5024]{1,0:T(2,128)S(1)}, f32[2,5024]{1,0:T(2,128)}, u32[]{:S(2)}) copy-start(f32[2,5024]{1,0:T(2,128)} %param.56) | copy-start | bytes 120580
  713.4 13.1 %copy-start.21 = (f32[2,5024]{1,0:T(2,128)S(1)}, f32[2,5024]{1,0:T(2,128)}, u32[]{:S(2)}) copy-start(f32[2,5024]{1,0:T(2,128)} %get-tuple-element.146) | copy-start | bytes 120580
  713.4 13.9 %copy-start.24 = (f32[32,160]{1,0:T(8,128)S(1)}, f32[32,160]{1,0:T(8,128)}, u32[]{:S(2)}) copy-start(f32[32,160]{1,0:T(8,128)} %param.40) | copy-start | bytes 61444
  713.4 13.9 %copy-start.25 = (f32[32,160]{1,0:T(8,128)S(1)}, f32[32,160]{1,0:T(8,128)}, u32[]{:S(2)}) copy-start(f32[32,160]{1,0:T(8,128)} %param.41) | copy-start | bytes 61444
  713.4 13.9 %copy-start.26 = (f32[32,160]{1,0:T(8,128)S(1)}, f32[32,160]{1,0:T(8,128)}, u32[]{:S(2)}) copy-start(f32[32,160]{1,0:T(8,128)} %get-tuple-element.139) | copy-start | bytes 61444
  713.4 14.5 %copy-start.30 = (f32[2049]{0:T(1024)S(1)}, f32[2049]{0:T(1024)}, u32[]{:S(2)}) copy-start(f32[2049]{0:T(1024)} %param.64) | copy-start | bytes 24592
  713.4 14.5 %copy-start.31 = (f32[2049]{0:T(1024)S(1)}, f32[2049]{0:T(1024)}, u32[]{:S(2)}) copy-start(f32[2049]{0:T(1024)} %param.65) | copy-start | bytes 24592
  713.4 15.1 %copy-start.32 = (f32[2,1280]{1,0:T(2,128)S(1)}, f32[2,1280]{1,0:T(2,128)}, u32[]{:S(2)}) copy-start(f32[2,1280]{1,0:T(2,128)} %param.58) | copy-start | bytes 30724
  713.4 15.1 %copy-start.33 = (f32[2,1280]{1,0:T(2,128)S(1)}, f32[2,1280]{1,0:T(2,128)}, u32[]{:S(2)}) copy-start(f32[2,1280]{1,0:T(2,128)} %param.59) | copy-start | bytes 30724
  713.5 15.1 %copy-start.34 = (f32[2,1280]{1,0:T(2,128)S(1)}, f32[2,1280]{1,0:T(2,128)}, u32[]{:S(2)}) copy-start(f32[2,1280]{1,0:T(2,128)} %get-tuple-element.147) | copy-start | bytes 30724
  713.5 15.8 %copy-start.23 = (f32[2048]{0:T(1024)S(1)}, f32[2048]{0:T(1024)}, u32[]{:S(2)}) copy-start(f32[2048]{0:T(1024)} %param.60) | copy-start | bytes 24580
  713.5 15.8 %copy-start.36 = (f32[2048]{0:T(1024)S(1)}, f32[2048]{0:T(1024)}, u32[]{:S(2)}) copy-start(f32[2048]{0:T(1024)} %param.61) | copy-start | bytes 24580
  713.5 15.7 %copy-start.37 = (f32[2048]{0:T(1024)S(1)}, f32[2048]{0:T(1024)}, u32[]{:S(2)}) copy-start(f32[2048]{0:T(1024)} %param.62) | copy-start | bytes 24580
  713.5 15.7 %copy-start.41 = (f32[1,2048]{1,0:T(1,128)S(1)}, f32[1,2048]{1,0:T(1,128)}, u32[]{:S(2)}) copy-start(f32[1,2048]{1,0:T(1,128)} %get-tuple-element.148) | copy-start | bytes 24580
  713.5 16.4 %copy-start.38 = (f32[2,928]{1,0:T(2,128)S(1)}, f32[2,928]{1,0:T(2,128)}, u32[]{:S(2)}) copy-start(f32[2,928]{1,0:T(2,128)} %param.52) | copy-start | bytes 22276
  713.5 16.4 %copy-start.39 = (f32[2,928]{1,0:T(2,128)S(1)}, f32[2,928]{1,0:T(2,128)}, u32[]{:S(2)}) copy-start(f32[2,928]{1,0:T(2,128)} %param.53) | copy-start | bytes 22276
  713.5 16.4 %copy-start.40 = (f32[2,928]{1,0:T(2,128)S(1)}, f32[2,928]{1,0:T(2,128)}, u32[]{:S(2)}) copy-start(f32[2,928]{1,0:T(2,128)} %get-tuple-element.145) | copy-start | bytes 22276
  713.5 17.0 %copy-start.2 = (f32[2,192,2560]{2,1,0:T(8,128)S(1)}, f32[2,192,2560]{2,1,0:T(8,128)}, u32[]{:S(2)}) copy-start(f32[2,192,2560]{2,1,0:T(8,128)} %param.45) | copy-start | bytes 11796484
  713.6 17.0 %copy-start.4 = (f32[2,192,2560]{2,1,0:T(8,128)S(1)}, f32[2,192,2560]{2,1,0:T(8,128)}, u32[]{:S(2)}) copy-start(f32[2,192,2560]{2,1,0:T(8,128)} %param.46) | copy-start | bytes 11796484
  713.6 17.0 %copy-start.5 = (f32[2,192,2560]{2,1,0:T(8,128)S(1)}, f32[2,192,2560]{2,1,0:T(8,128)}, u32[]{:S(2)}) copy-start(f32[2,192,2560]{2,1,0:T(8,128)} %param.47) | copy-start | bytes 11796484
  713.6 17.0 %copy-start.10 = (bf16[192,2560]{1,0:T(8,128)(2,1)S(1)}, bf16[192,2560]{1,0:T(8,128)(2,1)}, u32[]{:S(2)}) copy-start(bf16[192,2560]{1,0:T(8,128)(2,1)} %get-tuple-element.142) | copy-start | bytes 2949124
  713.6 17.0 %copy-start.11 = (bf16[192,2560]{1,0:T(8,128)(2,1)S(1)}, bf16[192,2560]{1,0:T(8,128)(2,1)}, u32[]{:S(2)}) copy-start(bf16[192,2560]{1,0:T(8,128)(2,1)} %get-tuple-element.143) | copy-start | bytes 2949124
  730.6 6.0 copy-start.6
  730.6 6.0 copy-start.7
  730.6 6.0 copy-start.13
  730.6 6.0 copy-start.14
